TPU v7x, 32 devices: a whole 2x2x4 slice. The times are simulated.
32 devices in a mesh: head: 2 (over x), ctx: 16 (over z, y, core).
Axes of the slice: x: 2, y: 2, z: 4, core: 2. Of those that a mesh axis runs over, the one named last changes fastest.
Arguments:
- queries: bfloat16 [2048, 1024], P(('head', 'ctx')), may hold values from -30 to 30
- key_vecs: bfloat16 [2048, 128], P(('head', 'ctx')), may hold values from -10 to 10
- value_vecs: bfloat16 [2048, 128], P(('head', 'ctx')), may hold values from -6 to 6
- out_grad: bfloat16 [2048, 1024], P(('head', 'ctx')), may hold values from -6 to 6
- positions: int32 [2048], P(('head', 'ctx')), may hold values from 0 to 2047, as said below
- documents: int32 [2048], P(('head', 'ctx')), may hold values from 0 to 2, as said below
Outputs:
- grad_queries: float32 [2048, 1024], P(('head', 'ctx'))
- grad_keys: float32 [2048, 128], P(('head', 'ctx'))
- grad_values: float32 [2048, 128], P(('head', 'ctx'))
Inputs may be any that keep to these rules, and one draw needn't show every extreme that they name: positions is a permutation of 0 to 2047; each aligned run of 64 rows holds 64 consecutive positions in rising order. `documents`: document ids never fall as positions rise, the token at position 0 has id 0, and every id up to the most occurs.
All inputs are finite; a program needn't handle non-finite values.
Results may differ from a plain program's by a relative error of at most 0.0059.
Values may be sent and summed in bfloat16 or wider, within the bound.
A program may use at most 64 MiB of HBM per device.

v0:
```python
import math

import jax
import jax.numpy as jnp
from jax import lax
from jax.sharding import PartitionSpec as P

NEG_BIG = -1e30


def from_behind(block, axis, distance):
    devices = range(lax.axis_size(axis))
    route = [((i - distance) % len(devices), i) for i in devices]
    return lax.ppermute(block, axis, route)


def block_visible(pos_query, doc_query, pos_key, doc_key):
    return (pos_key[None, :] <= pos_query[:, None]) & (doc_key[None, :] == doc_query[:, None])


def masked_scores(query_cube, key_rows, visible):
    inv_root = 1.0 / math.sqrt(query_cube.shape[-1])
    raw_scores = (
        jnp.einsum("thd,kd->thk", query_cube, key_rows, preferred_element_type=jnp.float32)
        * inv_root
    )
    return jnp.where(visible[:, None, :], raw_scores, NEG_BIG)


def stats_update(running, query_cube, grad_cube, key_rows, value_rows, visible):
    highest, denoms, cross_sum = running
    scores = masked_scores(query_cube, key_rows, visible)
    dprobs = jnp.einsum("thd,kd->thk", grad_cube, value_rows, preferred_element_type=jnp.float32)
    new_high = jnp.maximum(highest, jnp.max(scores, axis=2))
    weights = jnp.where(visible[:, None, :], jnp.exp(scores - new_high[:, :, None]), 0.0)
    return (new_high, jnp.sum(weights, axis=2), jnp.sum(weights * dprobs, axis=2))


def block_grads(query_cube, grad_cube, log_total, row_dot, key_rows, value_rows, visible):
    scores = masked_scores(query_cube, key_rows, visible)
    weights = jnp.where(visible[:, None, :], jnp.exp(scores - log_total[:, :, None]), 0.0)
    dprobs = jnp.einsum("thd,kd->thk", grad_cube, value_rows, preferred_element_type=jnp.float32)
    dscores = (weights * (dprobs - row_dot[:, :, None])).astype(jnp.bfloat16)
    return (weights.astype(jnp.bfloat16), dscores)


def query_part(dscores, key_rows):
    inv_root = 1.0 / math.sqrt(key_rows.shape[-1])
    return (
        jnp.einsum("thk,kd->thd", dscores, key_rows, preferred_element_type=jnp.float32) * inv_root
    )


def key_part(weights_b, dscores, query_cube, grad_cube):
    inv_root = 1.0 / math.sqrt(query_cube.shape[-1])
    key_grad = (
        jnp.einsum("thk,thd->kd", dscores, query_cube, preferred_element_type=jnp.float32)
        * inv_root
    )
    value_grad = jnp.einsum("thk,thd->kd", weights_b, grad_cube, preferred_element_type=jnp.float32)
    return jnp.concatenate([key_grad, value_grad], axis=1)


def on_device(queries, key_vecs, value_vecs, out_grad, positions, documents):
    head_count = lax.axis_size("head")
    ctx_count = lax.axis_size("ctx")
    ctx_here = lax.axis_index("ctx")
    head_dim = key_vecs.shape[1]
    query_tok, grad_tok = (
        lax.all_to_all(queries, "head", split_axis=1, concat_axis=0, tiled=True),
        lax.all_to_all(out_grad, "head", split_axis=1, concat_axis=0, tiled=True),
    )
    tok_rows = query_tok.shape[0]
    local_heads = query_tok.shape[1] // head_dim
    query_cube = query_tok.reshape(tok_rows, local_heads, head_dim)
    grad_cube = grad_tok.reshape(tok_rows, local_heads, head_dim)
    pos_all, doc_all = (
        lax.all_gather(positions, ("head", "ctx"), axis=0, tiled=True),
        lax.all_gather(documents, ("head", "ctx"), axis=0, tiled=True),
    )
    seq_len = pos_all.shape[0]
    shard_rows = seq_len // (head_count * ctx_count)
    pos_grid = pos_all.reshape(head_count, ctx_count, shard_rows)
    doc_grid = doc_all.reshape(head_count, ctx_count, shard_rows)
    pos_seq = jnp.transpose(pos_grid, (1, 0, 2)).reshape(seq_len)
    doc_seq = jnp.transpose(doc_grid, (1, 0, 2)).reshape(seq_len)

    def ctx_block(table, block_index):
        return lax.dynamic_index_in_dim(table, block_index, 1, keepdims=False).reshape(tok_rows)

    pos_own = ctx_block(pos_grid, ctx_here)
    doc_own = ctx_block(doc_grid, ctx_here)
    stat_zero = jnp.zeros((tok_rows, local_heads), jnp.float32)
    start_stats = (jnp.full((tok_rows, local_heads), NEG_BIG, jnp.float32), stat_zero, stat_zero)
    key_own, value_own = (
        lax.all_gather(key_vecs, "head", axis=0, tiled=True),
        lax.all_gather(value_vecs, "head", axis=0, tiled=True),
    )
    grad_zero = jnp.zeros((tok_rows, local_heads, head_dim), jnp.float32)
    pair_zero = jnp.zeros((tok_rows, 2 * head_dim), jnp.float32)
    key_rows = lax.all_gather(key_own, "ctx", axis=0, tiled=True)
    value_rows = lax.all_gather(value_own, "ctx", axis=0, tiled=True)
    visible = block_visible(pos_own, doc_own, pos_seq, doc_seq)
    highest, denoms, cross_sum = stats_update(
        start_stats, query_cube, grad_cube, key_rows, value_rows, visible
    )
    log_total = highest + jnp.log(denoms)
    row_dot = cross_sum / denoms

    def visit(step_no, state):
        query_blk, grad_blk, log_blk, dot_blk, qgrad_blk, key_grads = state
        block_index = (ctx_here - step_no) % ctx_count
        visible = block_visible(
            ctx_block(pos_grid, block_index), ctx_block(doc_grid, block_index), pos_own, doc_own
        )
        weights_b, dscores = block_grads(
            query_blk, grad_blk, log_blk, dot_blk, key_own, value_own, visible
        )
        qgrad_blk, key_grads = (
            qgrad_blk + query_part(dscores, key_own),
            key_grads + key_part(weights_b, dscores, query_blk, grad_blk),
        )
        return (query_blk, grad_blk, log_blk, dot_blk, qgrad_blk, key_grads)

    def advance(step_no, state):
        query_blk, grad_blk, log_blk, dot_blk, qgrad_blk, key_grads = visit(step_no, state)
        query_blk, grad_blk = from_behind((query_blk, grad_blk), "ctx", 1)
        log_blk, dot_blk, qgrad_blk = from_behind((log_blk, dot_blk, qgrad_blk), "ctx", 1)
        return (query_blk, grad_blk, log_blk, dot_blk, qgrad_blk, key_grads)

    state = (query_cube, grad_cube, log_total, row_dot, grad_zero, pair_zero)
    state = lax.fori_loop(0, ctx_count - 1, advance, state)
    state = visit(ctx_count - 1, state)
    grad_home = from_behind(state[4], "ctx", 1)
    key_grads = state[5]
    summed = lax.psum_scatter(key_grads, "head", scatter_dimension=0, tiled=True)
    grad_queries = lax.all_to_all(
        grad_home.reshape(tok_rows, local_heads * head_dim),
        "head",
        split_axis=0,
        concat_axis=1,
        tiled=True,
    )
    return (grad_queries, summed[:, :head_dim], summed[:, head_dim:])


def solution(mesh):
    placed = (
        P(("head", "ctx"), None),
        P(("head", "ctx"), None),
        P(("head", "ctx"), None),
        P(("head", "ctx"), None),
        P(("head", "ctx")),
        P(("head", "ctx")),
    )
    return jax.shard_map(
        on_device,
        mesh=mesh,
        in_specs=placed,
        out_specs=(P(("head", "ctx"), None), P(("head", "ctx"), None), P(("head", "ctx"), None)),
        check_vma=False,
    )
```

profile of v0, /device:TPU:0, one launch (start us, length us, event | category | flops | bytes accessed | tf_op | source)
XLA Modules:
  0.0 321.2 jit_solution(4248324950641893081)
XLA Ops:
  8.7 4.2 %all-to-all-start = ((bf16[64,2,512]{2,0,1:T(8,128)(2,1)}), bf16[64,2,512]{2,0,1:T(8,128)(2,1)S(1)}, u32[]{:S(2)}, u32[]{:S(2)}) async-start(bf16[64,2,512]{2,0,1:T(8,128)(2,1)} %bitcast.73), calls=%async_computation | async-start | bytes 262144 | tf_op jit(solution)/shard_map/all_to_all | solution.py:70
  14.6 41.8 %all-reduce.2 = (s32[2048]{0:T(1024)S(1)}, s32[2048]{0:T(1024)S(1)}) all-reduce(s32[2048]{0:T(1024)S(1)} %dynamic-update-slice.1, s32[2048]{0:T(1024)S(1)} %dynamic-update-slice), channel_id=1, replica_groups=mesh['head'=2,'ctx'=16] {'head','ctx'}, use_global_device_ids=true, to_apply=%add.1 | all-reduce | flops 4096 | bytes 32768
  58.1 4.9 %all_gather.20 = bf16[128,128]{1,0:T(8,128)(2,1)S(1)} all-gather(bf16[64,128]{1,0:T(8,128)(2,1)} %param.9), channel_id=1, replica_groups=mesh['head'=2,'ctx'=16] {'head'}, dimensions={0}, use_global_device_ids=true | all-gather | bytes 49152 | tf_op jit(solution)/shard_map/all_gather | solution.py:96
  63.1 22.2 %all_gather.21 = bf16[2048,128]{1,0:T(8,128)(2,1)S(1)} all-gather(bf16[128,128]{1,0:T(8,128)(2,1)S(1)} %all_gather.20), channel_id=1, replica_groups=mesh['head'=2,'ctx'=16] {'ctx'}, dimensions={0}, use_global_device_ids=true | all-gather | bytes 557056 | tf_op jit(solution)/shard_map/all_gather | solution.py:101
  85.2 4.6 %all_gather.22 = bf16[128,128]{1,0:T(8,128)(2,1)S(1)} all-gather(bf16[64,128]{1,0:T(8,128)(2,1)} %param.10), channel_id=1, replica_groups=mesh['head'=2,'ctx'=16] {'head'}, dimensions={0}, use_global_device_ids=true | all-gather | bytes 49152 | tf_op jit(solution)/shard_map/all_gather | solution.py:97
  90.1 18.7 %all_gather.23 = bf16[2048,128]{1,0:T(8,128)(2,1)S(1)} all-gather(bf16[128,128]{1,0:T(8,128)(2,1)S(1)} %all_gather.22), channel_id=1, replica_groups=mesh['head'=2,'ctx'=16] {'ctx'}, dimensions={0}, use_global_device_ids=true | all-gather | bytes 557056 | tf_op jit(solution)/shard_map/all_gather | solution.py:102
  110.5 3.4 %all-to-all-start.1 = ((bf16[64,2,512]{2,0,1:T(8,128)(2,1)}), bf16[64,2,512]{2,0,1:T(8,128)(2,1)S(1)}, u32[]{:S(2)}, u32[]{:S(2)}) async-start(bf16[64,2,512]{2,0,1:T(8,128)(2,1)} %bitcast.72), calls=%async_computation.1 | async-start | bytes 262144 | tf_op jit(solution)/shard_map/all_to_all | solution.py:71
  114.4 4.0 %all-to-all-done.1 = bf16[64,2,512]{2,0,1:T(8,128)(2,1)S(1)} async-done(((bf16[64,2,512]{2,0,1:T(8,128)(2,1)}), bf16[64,2,512]{2,0,1:T(8,128)(2,1)S(1)}, u32[]{:S(2)}, u32[]{:S(2)}) %all-to-all-start.1) | async-done | bytes 131104 | tf_op jit(solution)/shard_map/all_to_all | solution.py:71
  122.9 171.5 %while.27 = (s32[]{:T(128)}, bf16[128,4,128]{0,2,1:T(8,128)(2,1)S(1)}, bf16[128,4,128]{0,2,1:T(8,128)(2,1)S(1)}, f32[128,4]{0,1:T(4,128)S(1)}, f32[128,4]{0,1:T(...) while((s32[]{:T(128)}, ...), condition=%wide.wide.region_4.5_spmd.clone, body=%wide.wide.region_3.4_spmd.clone.sunk | while | flops 84705296 | bytes 5540390 | solution.py:132
  126.6 4.9 %collective-permute-done.2 = f32[128,4]{0,1:T(4,128)S(1)} collective-permute-done((f32[128,4]{0,1:T(4,128)S(1)}, f32[128,4]{0,1:T(4,128)S(1)}, u32[]{:S(2)}, u32[]{:S(2)}) %collective-permute-start.2) | collective-permute-done | bytes 2080 | tf_op jit(solution)/shard_map/while/body/eval_jaxpr/ppermute | solution.py:14
  131.6 3.1 collective-permute-done.4
  136.4 6.8 %collective-permute-done.2 = f32[128,4]{0,1:T(4,128)S(1)} collective-permute-done((f32[128,4]{0,1:T(4,128)S(1)}, f32[128,4]{0,1:T(4,128)S(1)}, u32[]{:S(2)}, u32[]{:S(2)}) %collective-permute-start.2) | collective-permute-done | bytes 2080 | tf_op jit(solution)/shard_map/while/body/eval_jaxpr/ppermute | solution.py:14
  143.3 2.8 collective-permute-done.4
  147.8 6.8 %collective-permute-done.2 = f32[128,4]{0,1:T(4,128)S(1)} collective-permute-done((f32[128,4]{0,1:T(4,128)S(1)}, f32[128,4]{0,1:T(4,128)S(1)}, u32[]{:S(2)}, u32[]{:S(2)}) %collective-permute-start.2) | collective-permute-done | bytes 2080 | tf_op jit(solution)/shard_map/while/body/eval_jaxpr/ppermute | solution.py:14
  159.8 6.3 %collective-permute-done.2 = f32[128,4]{0,1:T(4,128)S(1)} collective-permute-done((f32[128,4]{0,1:T(4,128)S(1)}, f32[128,4]{0,1:T(4,128)S(1)}, u32[]{:S(2)}, u32[]{:S(2)}) %collective-permute-start.2) | collective-permute-done | bytes 2080 | tf_op jit(solution)/shard_map/while/body/eval_jaxpr/ppermute | solution.py:14
  171.5 6.0 %collective-permute-done.2 = f32[128,4]{0,1:T(4,128)S(1)} collective-permute-done((f32[128,4]{0,1:T(4,128)S(1)}, f32[128,4]{0,1:T(4,128)S(1)}, u32[]{:S(2)}, u32[]{:S(2)}) %collective-permute-start.2) | collective-permute-done | bytes 2080 | tf_op jit(solution)/shard_map/while/body/eval_jaxpr/ppermute | solution.py:14
  182.9 6.0 %collective-permute-done.2 = f32[128,4]{0,1:T(4,128)S(1)} collective-permute-done((f32[128,4]{0,1:T(4,128)S(1)}, f32[128,4]{0,1:T(4,128)S(1)}, u32[]{:S(2)}, u32[]{:S(2)}) %collective-permute-start.2) | collective-permute-done | bytes 2080 | tf_op jit(solution)/shard_map/while/body/eval_jaxpr/ppermute | solution.py:14
  194.3 6.0 %collective-permute-done.2 = f32[128,4]{0,1:T(4,128)S(1)} collective-permute-done((f32[128,4]{0,1:T(4,128)S(1)}, f32[128,4]{0,1:T(4,128)S(1)}, u32[]{:S(2)}, u32[]{:S(2)}) %collective-permute-start.2) | collective-permute-done | bytes 2080 | tf_op jit(solution)/shard_map/while/body/eval_jaxpr/ppermute | solution.py:14
  205.7 6.0 %collective-permute-done.2 = f32[128,4]{0,1:T(4,128)S(1)} collective-permute-done((f32[128,4]{0,1:T(4,128)S(1)}, f32[128,4]{0,1:T(4,128)S(1)}, u32[]{:S(2)}, u32[]{:S(2)}) %collective-permute-start.2) | collective-permute-done | bytes 2080 | tf_op jit(solution)/shard_map/while/body/eval_jaxpr/ppermute | solution.py:14
  217.1 6.0 %collective-permute-done.2 = f32[128,4]{0,1:T(4,128)S(1)} collective-permute-done((f32[128,4]{0,1:T(4,128)S(1)}, f32[128,4]{0,1:T(4,128)S(1)}, u32[]{:S(2)}, u32[]{:S(2)}) %collective-permute-start.2) | collective-permute-done | bytes 2080 | tf_op jit(solution)/shard_map/while/body/eval_jaxpr/ppermute | solution.py:14
  223.2 2.8 collective-permute-done.4
  228.5 6.0 %collective-permute-done.2 = f32[128,4]{0,1:T(4,128)S(1)} collective-permute-done((f32[128,4]{0,1:T(4,128)S(1)}, f32[128,4]{0,1:T(4,128)S(1)}, u32[]{:S(2)}, u32[]{:S(2)}) %collective-permute-start.2) | collective-permute-done | bytes 2080 | tf_op jit(solution)/shard_map/while/body/eval_jaxpr/ppermute | solution.py:14
  234.6 2.8 collective-permute-done.4
  240.0 6.0 %collective-permute-done.2 = f32[128,4]{0,1:T(4,128)S(1)} collective-permute-done((f32[128,4]{0,1:T(4,128)S(1)}, f32[128,4]{0,1:T(4,128)S(1)}, u32[]{:S(2)}, u32[]{:S(2)}) %collective-permute-start.2) | collective-permute-done | bytes 2080 | tf_op jit(solution)/shard_map/while/body/eval_jaxpr/ppermute | solution.py:14
  246.0 2.8 collective-permute-done.4
  251.4 6.0 %collective-permute-done.2 = f32[128,4]{0,1:T(4,128)S(1)} collective-permute-done((f32[128,4]{0,1:T(4,128)S(1)}, f32[128,4]{0,1:T(4,128)S(1)}, u32[]{:S(2)}, u32[]{:S(2)}) %collective-permute-start.2) | collective-permute-done | bytes 2080 | tf_op jit(solution)/shard_map/while/body/eval_jaxpr/ppermute | solution.py:14
  262.8 6.0 %collective-permute-done.2 = f32[128,4]{0,1:T(4,128)S(1)} collective-permute-done((f32[128,4]{0,1:T(4,128)S(1)}, f32[128,4]{0,1:T(4,128)S(1)}, u32[]{:S(2)}, u32[]{:S(2)}) %collective-permute-start.2) | collective-permute-done | bytes 2080 | tf_op jit(solution)/shard_map/while/body/eval_jaxpr/ppermute | solution.py:14
  274.2 6.0 %collective-permute-done.2 = f32[128,4]{0,1:T(4,128)S(1)} collective-permute-done((f32[128,4]{0,1:T(4,128)S(1)}, f32[128,4]{0,1:T(4,128)S(1)}, u32[]{:S(2)}, u32[]{:S(2)}) %collective-permute-start.2) | collective-permute-done | bytes 2080 | tf_op jit(solution)/shard_map/while/body/eval_jaxpr/ppermute | solution.py:14
  285.6 6.0 %collective-permute-done.2 = f32[128,4]{0,1:T(4,128)S(1)} collective-permute-done((f32[128,4]{0,1:T(4,128)S(1)}, f32[128,4]{0,1:T(4,128)S(1)}, u32[]{:S(2)}, u32[]{:S(2)}) %collective-permute-start.2) | collective-permute-done | bytes 2080 | tf_op jit(solution)/shard_map/while/body/eval_jaxpr/ppermute | solution.py:14
  296.3 7.7 %collective-permute-done.5 = f32[128,4,128]{2,0,1:T(8,128)S(1)} collective-permute-done((f32[128,4,128]{2,0,1:T(8,128)S(1)}, f32[128,4,128]{2,0,1:T(8,128)S(1)}, u32[]{:S(2)}, u32[]{:S(2)}) %collective-permute-start.5) | collective-permute-done | bytes 262176 | tf_op jit(solution)/shard_map/ppermute | solution.py:14
  305.0 3.4 %all-to-all-start.2 = ((f32[2,64,512]{2,1,0:T(8,128)}), f32[2,64,512]{2,1,0:T(8,128)S(1)}, u32[]{:S(2)}, u32[]{:S(2)}) async-start(f32[2,64,512]{2,1,0:T(8,128)} %all_to_all.44), calls=%async_computation.2 | async-start | bytes 524288 | tf_op jit(solution)/shard_map/all_to_all | solution.py:137
  309.9 3.7 %all-to-all-done.2 = f32[2,64,512]{2,1,0:T(8,128)S(1)} async-done(((f32[2,64,512]{2,1,0:T(8,128)}), f32[2,64,512]{2,1,0:T(8,128)S(1)}, u32[]{:S(2)}, u32[]{:S(2)}) %all-to-all-start.2) | async-done | bytes 262176 | tf_op jit(solution)/shard_map/all_to_all | solution.py:137
  (393 shorter events, 81.4 us)
Async XLA Ops:
  8.7 101.8 %all-to-all-start = ((bf16[64,2,512]{2,0,1:T(8,128)(2,1)}), bf16[64,2,512]{2,0,1:T(8,128)(2,1)S(1)}, u32[]{:S(2)}, u32[]{:S(2)}) async-start(bf16[64,2,512]{2,0,1:T(8,128)(2,1)} %bitcast.73), calls=%async_computation | async-start | bytes 262144 | tf_op jit(solution)/shard_map/all_to_all | solution.py:70
  113.9 194.5 %reduce-scatter.4.cloned.1.call-start = ((), (), s32[]{:S(2)}) async-start(), calls=%async_computation.4 | async-start | bytes 196608
  123.0 8.6 %collective-permute-start = (bf16[128,4,128]{0,2,1:T(8,128)(2,1)S(1)}, bf16[128,4,128]{0,2,1:T(8,128)(2,1)S(1)}, u32[]{:S(2)}, u32[]{:S(2)}) collective-permute-start(bf16[128,4,128]{0,2,1:T(8,128)(2,1)S(1)} %copy.95), channel_id=1, source_target_pairs={{15,0},{0,1},{1,2},{2,3},{3,4},{4,5},{5,6},{6,7},{7,8},{8,9},{9,10... | collective-permute-start | bytes 393224 | tf_op jit(solution)/shard_map/while/body/eval_jaxpr/ppermute | solution.py:14
  134.7 8.6 %collective-permute-start = (bf16[128,4,128]{0,2,1:T(8,128)(2,1)S(1)}, bf16[128,4,128]{0,2,1:T(8,128)(2,1)S(1)}, u32[]{:S(2)}, u32[]{:S(2)}) collective-permute-start(bf16[128,4,128]{0,2,1:T(8,128)(2,1)S(1)} %copy.95), channel_id=1, source_target_pairs={{15,0},{0,1},{1,2},{2,3},{3,4},{4,5},{5,6},{6,7},{7,8},{8,9},{9,10... | collective-permute-start | bytes 393224 | tf_op jit(solution)/shard_map/while/body/eval_jaxpr/ppermute | solution.py:14
  135.9 10.1 %collective-permute-start.4 = (f32[128,4,128]{2,0,1:T(8,128)S(1)}, f32[128,4,128]{2,0,1:T(8,128)S(1)}, u32[]{:S(2)}, u32[]{:S(2)}) collective-permute-start(f32[128,4,128]{2,0,1:T(8,128)S(1)} %fusion.87), channel_id=1, source_target_pairs={{15,0},{0,1},{1,2},{2,3},{3,4},{4,5},{5,6},{6,7},{7,8},{8,9},{9,10... | collective-permute-start | bytes 786440 | tf_op jit(solution)/shard_map/while/body/eval_jaxpr/ppermute | solution.py:14
  146.1 8.6 %collective-permute-start = (bf16[128,4,128]{0,2,1:T(8,128)(2,1)S(1)}, bf16[128,4,128]{0,2,1:T(8,128)(2,1)S(1)}, u32[]{:S(2)}, u32[]{:S(2)}) collective-permute-start(bf16[128,4,128]{0,2,1:T(8,128)(2,1)S(1)} %copy.95), channel_id=1, source_target_pairs={{15,0},{0,1},{1,2},{2,3},{3,4},{4,5},{5,6},{6,7},{7,8},{8,9},{9,10... | collective-permute-start | bytes 393224 | tf_op jit(solution)/shard_map/while/body/eval_jaxpr/ppermute | solution.py:14
  147.4 10.1 %collective-permute-start.4 = (f32[128,4,128]{2,0,1:T(8,128)S(1)}, f32[128,4,128]{2,0,1:T(8,128)S(1)}, u32[]{:S(2)}, u32[]{:S(2)}) collective-permute-start(f32[128,4,128]{2,0,1:T(8,128)S(1)} %fusion.87), channel_id=1, source_target_pairs={{15,0},{0,1},{1,2},{2,3},{3,4},{4,5},{5,6},{6,7},{7,8},{8,9},{9,10... | collective-permute-start | bytes 786440 | tf_op jit(solution)/shard_map/while/body/eval_jaxpr/ppermute | solution.py:14
  157.5 8.6 %collective-permute-start = (bf16[128,4,128]{0,2,1:T(8,128)(2,1)S(1)}, bf16[128,4,128]{0,2,1:T(8,128)(2,1)S(1)}, u32[]{:S(2)}, u32[]{:S(2)}) collective-permute-start(bf16[128,4,128]{0,2,1:T(8,128)(2,1)S(1)} %copy.95), channel_id=1, source_target_pairs={{15,0},{0,1},{1,2},{2,3},{3,4},{4,5},{5,6},{6,7},{7,8},{8,9},{9,10... | collective-permute-start | bytes 393224 | tf_op jit(solution)/shard_map/while/body/eval_jaxpr/ppermute | solution.py:14
  159.2 9.7 %collective-permute-start.4 = (f32[128,4,128]{2,0,1:T(8,128)S(1)}, f32[128,4,128]{2,0,1:T(8,128)S(1)}, u32[]{:S(2)}, u32[]{:S(2)}) collective-permute-start(f32[128,4,128]{2,0,1:T(8,128)S(1)} %fusion.87), channel_id=1, source_target_pairs={{15,0},{0,1},{1,2},{2,3},{3,4},{4,5},{5,6},{6,7},{7,8},{8,9},{9,10... | collective-permute-start | bytes 786440 | tf_op jit(solution)/shard_map/while/body/eval_jaxpr/ppermute | solution.py:14
  168.9 8.6 %collective-permute-start = (bf16[128,4,128]{0,2,1:T(8,128)(2,1)S(1)}, bf16[128,4,128]{0,2,1:T(8,128)(2,1)S(1)}, u32[]{:S(2)}, u32[]{:S(2)}) collective-permute-start(bf16[128,4,128]{0,2,1:T(8,128)(2,1)S(1)} %copy.95), channel_id=1, source_target_pairs={{15,0},{0,1},{1,2},{2,3},{3,4},{4,5},{5,6},{6,7},{7,8},{8,9},{9,10... | collective-permute-start | bytes 393224 | tf_op jit(solution)/shard_map/while/body/eval_jaxpr/ppermute | solution.py:14
  170.9 9.4 %collective-permute-start.4 = (f32[128,4,128]{2,0,1:T(8,128)S(1)}, f32[128,4,128]{2,0,1:T(8,128)S(1)}, u32[]{:S(2)}, u32[]{:S(2)}) collective-permute-start(f32[128,4,128]{2,0,1:T(8,128)S(1)} %fusion.87), channel_id=1, source_target_pairs={{15,0},{0,1},{1,2},{2,3},{3,4},{4,5},{5,6},{6,7},{7,8},{8,9},{9,10... | collective-permute-start | bytes 786440 | tf_op jit(solution)/shard_map/while/body/eval_jaxpr/ppermute | solution.py:14
  180.3 8.6 %collective-permute-start = (bf16[128,4,128]{0,2,1:T(8,128)(2,1)S(1)}, bf16[128,4,128]{0,2,1:T(8,128)(2,1)S(1)}, u32[]{:S(2)}, u32[]{:S(2)}) collective-permute-start(bf16[128,4,128]{0,2,1:T(8,128)(2,1)S(1)} %copy.95), channel_id=1, source_target_pairs={{15,0},{0,1},{1,2},{2,3},{3,4},{4,5},{5,6},{6,7},{7,8},{8,9},{9,10... | collective-permute-start | bytes 393224 | tf_op jit(solution)/shard_map/while/body/eval_jaxpr/ppermute | solution.py:14
  182.3 9.4 %collective-permute-start.4 = (f32[128,4,128]{2,0,1:T(8,128)S(1)}, f32[128,4,128]{2,0,1:T(8,128)S(1)}, u32[]{:S(2)}, u32[]{:S(2)}) collective-permute-start(f32[128,4,128]{2,0,1:T(8,128)S(1)} %fusion.87), channel_id=1, source_target_pairs={{15,0},{0,1},{1,2},{2,3},{3,4},{4,5},{5,6},{6,7},{7,8},{8,9},{9,10... | collective-permute-start | bytes 786440 | tf_op jit(solution)/shard_map/while/body/eval_jaxpr/ppermute | solution.py:14
  191.7 8.6 %collective-permute-start = (bf16[128,4,128]{0,2,1:T(8,128)(2,1)S(1)}, bf16[128,4,128]{0,2,1:T(8,128)(2,1)S(1)}, u32[]{:S(2)}, u32[]{:S(2)}) collective-permute-start(bf16[128,4,128]{0,2,1:T(8,128)(2,1)S(1)} %copy.95), channel_id=1, source_target_pairs={{15,0},{0,1},{1,2},{2,3},{3,4},{4,5},{5,6},{6,7},{7,8},{8,9},{9,10... | collective-permute-start | bytes 393224 | tf_op jit(solution)/shard_map/while/body/eval_jaxpr/ppermute | solution.py:14
  193.8 9.4 %collective-permute-start.4 = (f32[128,4,128]{2,0,1:T(8,128)S(1)}, f32[128,4,128]{2,0,1:T(8,128)S(1)}, u32[]{:S(2)}, u32[]{:S(2)}) collective-permute-start(f32[128,4,128]{2,0,1:T(8,128)S(1)} %fusion.87), channel_id=1, source_target_pairs={{15,0},{0,1},{1,2},{2,3},{3,4},{4,5},{5,6},{6,7},{7,8},{8,9},{9,10... | collective-permute-start | bytes 786440 | tf_op jit(solution)/shard_map/while/body/eval_jaxpr/ppermute | solution.py:14
  203.1 8.6 %collective-permute-start = (bf16[128,4,128]{0,2,1:T(8,128)(2,1)S(1)}, bf16[128,4,128]{0,2,1:T(8,128)(2,1)S(1)}, u32[]{:S(2)}, u32[]{:S(2)}) collective-permute-start(bf16[128,4,128]{0,2,1:T(8,128)(2,1)S(1)} %copy.95), channel_id=1, source_target_pairs={{15,0},{0,1},{1,2},{2,3},{3,4},{4,5},{5,6},{6,7},{7,8},{8,9},{9,10... | collective-permute-start | bytes 393224 | tf_op jit(solution)/shard_map/while/body/eval_jaxpr/ppermute | solution.py:14
  205.2 9.4 %collective-permute-start.4 = (f32[128,4,128]{2,0,1:T(8,128)S(1)}, f32[128,4,128]{2,0,1:T(8,128)S(1)}, u32[]{:S(2)}, u32[]{:S(2)}) collective-permute-start(f32[128,4,128]{2,0,1:T(8,128)S(1)} %fusion.87), channel_id=1, source_target_pairs={{15,0},{0,1},{1,2},{2,3},{3,4},{4,5},{5,6},{6,7},{7,8},{8,9},{9,10... | collective-permute-start | bytes 786440 | tf_op jit(solution)/shard_map/while/body/eval_jaxpr/ppermute | solution.py:14
  214.6 8.6 %collective-permute-start = (bf16[128,4,128]{0,2,1:T(8,128)(2,1)S(1)}, bf16[128,4,128]{0,2,1:T(8,128)(2,1)S(1)}, u32[]{:S(2)}, u32[]{:S(2)}) collective-permute-start(bf16[128,4,128]{0,2,1:T(8,128)(2,1)S(1)} %copy.95), channel_id=1, source_target_pairs={{15,0},{0,1},{1,2},{2,3},{3,4},{4,5},{5,6},{6,7},{7,8},{8,9},{9,10... | collective-permute-start | bytes 393224 | tf_op jit(solution)/shard_map/while/body/eval_jaxpr/ppermute | solution.py:14
  216.6 9.4 %collective-permute-start.4 = (f32[128,4,128]{2,0,1:T(8,128)S(1)}, f32[128,4,128]{2,0,1:T(8,128)S(1)}, u32[]{:S(2)}, u32[]{:S(2)}) collective-permute-start(f32[128,4,128]{2,0,1:T(8,128)S(1)} %fusion.87), channel_id=1, source_target_pairs={{15,0},{0,1},{1,2},{2,3},{3,4},{4,5},{5,6},{6,7},{7,8},{8,9},{9,10... | collective-permute-start | bytes 786440 | tf_op jit(solution)/shard_map/while/body/eval_jaxpr/ppermute | solution.py:14
  226.0 8.6 %collective-permute-start = (bf16[128,4,128]{0,2,1:T(8,128)(2,1)S(1)}, bf16[128,4,128]{0,2,1:T(8,128)(2,1)S(1)}, u32[]{:S(2)}, u32[]{:S(2)}) collective-permute-start(bf16[128,4,128]{0,2,1:T(8,128)(2,1)S(1)} %copy.95), channel_id=1, source_target_pairs={{15,0},{0,1},{1,2},{2,3},{3,4},{4,5},{5,6},{6,7},{7,8},{8,9},{9,10... | collective-permute-start | bytes 393224 | tf_op jit(solution)/shard_map/while/body/eval_jaxpr/ppermute | solution.py:14
  228.0 9.4 %collective-permute-start.4 = (f32[128,4,128]{2,0,1:T(8,128)S(1)}, f32[128,4,128]{2,0,1:T(8,128)S(1)}, u32[]{:S(2)}, u32[]{:S(2)}) collective-permute-start(f32[128,4,128]{2,0,1:T(8,128)S(1)} %fusion.87), channel_id=1, source_target_pairs={{15,0},{0,1},{1,2},{2,3},{3,4},{4,5},{5,6},{6,7},{7,8},{8,9},{9,10... | collective-permute-start | bytes 786440 | tf_op jit(solution)/shard_map/while/body/eval_jaxpr/ppermute | solution.py:14
  237.4 8.6 %collective-permute-start = (bf16[128,4,128]{0,2,1:T(8,128)(2,1)S(1)}, bf16[128,4,128]{0,2,1:T(8,128)(2,1)S(1)}, u32[]{:S(2)}, u32[]{:S(2)}) collective-permute-start(bf16[128,4,128]{0,2,1:T(8,128)(2,1)S(1)} %copy.95), channel_id=1, source_target_pairs={{15,0},{0,1},{1,2},{2,3},{3,4},{4,5},{5,6},{6,7},{7,8},{8,9},{9,10... | collective-permute-start | bytes 393224 | tf_op jit(solution)/shard_map/while/body/eval_jaxpr/ppermute | solution.py:14
  239.4 9.4 %collective-permute-start.4 = (f32[128,4,128]{2,0,1:T(8,128)S(1)}, f32[128,4,128]{2,0,1:T(8,128)S(1)}, u32[]{:S(2)}, u32[]{:S(2)}) collective-permute-start(f32[128,4,128]{2,0,1:T(8,128)S(1)} %fusion.87), channel_id=1, source_target_pairs={{15,0},{0,1},{1,2},{2,3},{3,4},{4,5},{5,6},{6,7},{7,8},{8,9},{9,10... | collective-permute-start | bytes 786440 | tf_op jit(solution)/shard_map/while/body/eval_jaxpr/ppermute | solution.py:14
  248.8 8.6 %collective-permute-start = (bf16[128,4,128]{0,2,1:T(8,128)(2,1)S(1)}, bf16[128,4,128]{0,2,1:T(8,128)(2,1)S(1)}, u32[]{:S(2)}, u32[]{:S(2)}) collective-permute-start(bf16[128,4,128]{0,2,1:T(8,128)(2,1)S(1)} %copy.95), channel_id=1, source_target_pairs={{15,0},{0,1},{1,2},{2,3},{3,4},{4,5},{5,6},{6,7},{7,8},{8,9},{9,10... | collective-permute-start | bytes 393224 | tf_op jit(solution)/shard_map/while/body/eval_jaxpr/ppermute | solution.py:14
  250.8 9.4 %collective-permute-start.4 = (f32[128,4,128]{2,0,1:T(8,128)S(1)}, f32[128,4,128]{2,0,1:T(8,128)S(1)}, u32[]{:S(2)}, u32[]{:S(2)}) collective-permute-start(f32[128,4,128]{2,0,1:T(8,128)S(1)} %fusion.87), channel_id=1, source_target_pairs={{15,0},{0,1},{1,2},{2,3},{3,4},{4,5},{5,6},{6,7},{7,8},{8,9},{9,10... | collective-permute-start | bytes 786440 | tf_op jit(solution)/shard_map/while/body/eval_jaxpr/ppermute | solution.py:14
  260.2 8.6 %collective-permute-start = (bf16[128,4,128]{0,2,1:T(8,128)(2,1)S(1)}, bf16[128,4,128]{0,2,1:T(8,128)(2,1)S(1)}, u32[]{:S(2)}, u32[]{:S(2)}) collective-permute-start(bf16[128,4,128]{0,2,1:T(8,128)(2,1)S(1)} %copy.95), channel_id=1, source_target_pairs={{15,0},{0,1},{1,2},{2,3},{3,4},{4,5},{5,6},{6,7},{7,8},{8,9},{9,10... | collective-permute-start | bytes 393224 | tf_op jit(solution)/shard_map/while/body/eval_jaxpr/ppermute | solution.py:14
  262.2 9.4 %collective-permute-start.4 = (f32[128,4,128]{2,0,1:T(8,128)S(1)}, f32[128,4,128]{2,0,1:T(8,128)S(1)}, u32[]{:S(2)}, u32[]{:S(2)}) collective-permute-start(f32[128,4,128]{2,0,1:T(8,128)S(1)} %fusion.87), channel_id=1, source_target_pairs={{15,0},{0,1},{1,2},{2,3},{3,4},{4,5},{5,6},{6,7},{7,8},{8,9},{9,10... | collective-permute-start | bytes 786440 | tf_op jit(solution)/shard_map/while/body/eval_jaxpr/ppermute | solution.py:14
  271.6 8.6 %collective-permute-start = (bf16[128,4,128]{0,2,1:T(8,128)(2,1)S(1)}, bf16[128,4,128]{0,2,1:T(8,128)(2,1)S(1)}, u32[]{:S(2)}, u32[]{:S(2)}) collective-permute-start(bf16[128,4,128]{0,2,1:T(8,128)(2,1)S(1)} %copy.95), channel_id=1, source_target_pairs={{15,0},{0,1},{1,2},{2,3},{3,4},{4,5},{5,6},{6,7},{7,8},{8,9},{9,10... | collective-permute-start | bytes 393224 | tf_op jit(solution)/shard_map/while/body/eval_jaxpr/ppermute | solution.py:14
  273.7 9.4 %collective-permute-start.4 = (f32[128,4,128]{2,0,1:T(8,128)S(1)}, f32[128,4,128]{2,0,1:T(8,128)S(1)}, u32[]{:S(2)}, u32[]{:S(2)}) collective-permute-start(f32[128,4,128]{2,0,1:T(8,128)S(1)} %fusion.87), channel_id=1, source_target_pairs={{15,0},{0,1},{1,2},{2,3},{3,4},{4,5},{5,6},{6,7},{7,8},{8,9},{9,10... | collective-permute-start | bytes 786440 | tf_op jit(solution)/shard_map/while/body/eval_jaxpr/ppermute | solution.py:14
  283.0 8.6 %collective-permute-start = (bf16[128,4,128]{0,2,1:T(8,128)(2,1)S(1)}, bf16[128,4,128]{0,2,1:T(8,128)(2,1)S(1)}, u32[]{:S(2)}, u32[]{:S(2)}) collective-permute-start(bf16[128,4,128]{0,2,1:T(8,128)(2,1)S(1)} %copy.95), channel_id=1, source_target_pairs={{15,0},{0,1},{1,2},{2,3},{3,4},{4,5},{5,6},{6,7},{7,8},{8,9},{9,10... | collective-permute-start | bytes 393224 | tf_op jit(solution)/shard_map/while/body/eval_jaxpr/ppermute | solution.py:14
  285.1 9.4 %collective-permute-start.4 = (f32[128,4,128]{2,0,1:T(8,128)S(1)}, f32[128,4,128]{2,0,1:T(8,128)S(1)}, u32[]{:S(2)}, u32[]{:S(2)}) collective-permute-start(f32[128,4,128]{2,0,1:T(8,128)S(1)} %fusion.87), channel_id=1, source_target_pairs={{15,0},{0,1},{1,2},{2,3},{3,4},{4,5},{5,6},{6,7},{7,8},{8,9},{9,10... | collective-permute-start | bytes 786440 | tf_op jit(solution)/shard_map/while/body/eval_jaxpr/ppermute | solution.py:14
  305.0 8.6 %all-to-all-start.2 = ((f32[2,64,512]{2,1,0:T(8,128)}), f32[2,64,512]{2,1,0:T(8,128)S(1)}, u32[]{:S(2)}, u32[]{:S(2)}) async-start(f32[2,64,512]{2,1,0:T(8,128)} %all_to_all.44), calls=%async_computation.2 | async-start | bytes 524288 | tf_op jit(solution)/shard_map/all_to_all | solution.py:137
  (50 other events, 526.4 us)
Sparse Core Ops, SparseCore 0:
  296.4 11.1 reduce-scatter.3
where the time goes:
time: 322 us; the launch traced here: 321 us
  waiting for transfers between devices  149 us (46%)
  blocking collectives  92.2 us (29%)
  starting transfers between devices  27.5 us (9%)
  matrix products  18.7 us (6%)
  between operations  14.2 us (4%)
  local copies, waits for them, and re-layouts  14 us (4%)
  other arithmetic  3.74 us (1%)
    ppermute x76, waiting for transfers between devices, from_behind(): return lax.ppermute(block, axis, route)  141 us
    unnamed x1, blocking collectives  41.8 us
    all_gather x1, blocking collectives, on_device(): key_rows = lax.all_gather(key_own, 'ctx', axis=0, tiled=True)  22.2 us
    all_gather x1, blocking collectives, on_device(): value_rows = lax.all_gather(value_own, 'ctx', axis=0, tiled=True)  18.7 us
    ppermute x76, starting transfers between devices, from_behind(): return lax.ppermute(block, axis, route)  16.4 us
  transfers between devices with their start and end apart: 80, of which 33 were waited for; matrix products, arithmetic and copies ran while one was open for 9% of the time, Pallas kernels for 0%

commit v1 on v0

v1 whole, which is shorter than its diff:
```python
import functools
import math

import jax
import jax.numpy as jnp
from jax import lax
from jax.experimental import pallas as pl
from jax.experimental.pallas import tpu as pltpu
from jax.sharding import PartitionSpec as P

MESH = pl.DeviceIdType.MESH
NEG_BIG = -1e30
CORES = 2
SIDES = 2
F32 = jnp.float32
BF16 = jnp.bfloat16


def dot(lhs, rhs, lhs_dim, rhs_dim):
    return lax.dot_general(
        lhs, rhs, (((lhs_dim,), (rhs_dim,)), ((), ())), preferred_element_type=F32
    )


def kernel(
    cfg,
    q_ref, k_ref, v_ref, g_ref, pos_ref, doc_ref,
    dq_ref, dk_ref, dv_ref,
    qs, gs, kv, info, sbuf, dpbuf, top, den, cross, dqt, acck, accv,
    core_out, core_in, yk_out, yk_in, xv_out, xv_in, xk_out, xk_in, yv_out, yv_in,
    a_out, a_in, a_own, *sems,
):
    nx, na, rows, heads, docs = cfg
    chunk = na * rows
    lanes = heads * rows
    half = SIDES * nx
    inv_root = 1.0 / math.sqrt(128)
    scale = inv_root * math.log2(math.e)

    x = lax.axis_index("head")
    ctx = lax.axis_index("ctx")
    a, y, c = ctx // 4, (ctx // 2) % 2, ctx % 2

    def device(a_=None, y_=None, c_=None, x_=None):
        a_ = a if a_ is None else a_
        y_ = y if y_ is None else y_
        c_ = c if c_ is None else c_
        return (x if x_ is None else x_, a_ * 4 + y_ * 2 + c_)

    a_peers = [device(a_=(a + r) % na) for r in range(1, na)]
    x_peers = [device(x_=(x + r) % nx) for r in range(1, nx)]
    y_peer = device(y_=1 - y)
    c_peer = device(c_=1 - c)

    (s_akv, r_akv, s_ainf, r_ainf, s_xkv, r_xkv, s_xinf, r_xinf, s_ykv, r_ykv, s_yinf, r_yinf,
     s_fk, r_fk, s_finf, r_finf, s_fv, r_fv, s_ckv, r_ckv, s_cinf, r_cinf,
     s_rc, r_rc, s_k1, r_k1, s_v1, r_v1, s_k2, r_k2, s_v2, r_v2, s_ra, r_ra) = sems

    def copy(src, dst, send, recv, to):
        return pltpu.make_async_remote_copy(
            src_ref=src, dst_ref=dst, send_sem=send, recv_sem=recv, device_id=to, device_id_type=MESH
        )

    barrier = pltpu.get_barrier_semaphore()
    everyone = a_peers + x_peers + [y_peer, c_peer]
    for to in everyone:
        pl.semaphore_signal(barrier, inc=1, device_id=to, device_id_type=MESH)

    own_rows = pl.ds(pl.multiple_of(a * rows, rows), rows)
    kv[c, y, x, 0, own_rows, :] = k_ref[...]
    kv[c, y, x, 1, own_rows, :] = v_ref[...]
    fields = docs + 1
    own_info = a * fields
    pos_own = pos_ref[...]
    doc_own = doc_ref[...]
    info[c, y, x, own_info] = jnp.broadcast_to(pos_own[:, 0:1], (1, 128))
    for d in range(docs):
        tally = jnp.sum(jnp.where(doc_own == d, 1, 0), axis=1, keepdims=True)
        info[c, y, x, own_info + 1 + d] = jnp.broadcast_to(tally, (1, 128))

    pl.semaphore_wait(barrier, len(everyone))

    def a_kv(i):
        block = kv.at[c, y, x, :, own_rows, :]
        return copy(block, block, s_akv.at[i], r_akv.at[i], a_peers[i])

    def a_inf(i):
        block = info.at[c, y, x, pl.ds(own_info, fields)]
        return copy(block, block, s_ainf.at[i], r_ainf.at[i], a_peers[i])

    gather = [a_kv(i) for i in range(na - 1)] + [a_inf(i) for i in range(na - 1)]
    for one in gather:
        one.start()

    for h in range(heads):
        qs[h * rows : (h + 1) * rows, :] = q_ref[:, h * 128 : (h + 1) * 128]
        gs[h * rows : (h + 1) * rows, :] = g_ref[:, h * 128 : (h + 1) * 128]
    pos_q = jnp.concatenate([pos_own] * heads, axis=1)
    doc_q = jnp.concatenate([doc_own] * heads, axis=1)
    top[...] = jnp.full(top.shape, NEG_BIG, F32)
    den[...] = jnp.zeros(den.shape, F32)
    cross[...] = jnp.zeros(cross.shape, F32)
    dqt[...] = jnp.zeros(dqt.shape, F32)
    for one in gather:
        one.wait_recv()

    mine = kv.at[c, y, x]
    mine_info = info.at[c, y, x]
    direct = []
    for i in range(nx - 1):
        direct.append(copy(mine, mine, s_xkv.at[i], r_xkv.at[i], x_peers[i]))
        direct.append(copy(mine_info, mine_info, s_xinf.at[i], r_xinf.at[i], x_peers[i]))
    direct.append(copy(mine, mine, s_ykv, r_ykv, y_peer))
    direct.append(copy(mine_info, mine_info, s_yinf, r_yinf, y_peer))

    def place(step):
        return ((c + step // half) % CORES, (y + (step // nx) % SIDES) % SIDES, (x + step % nx) % nx)

    def to_core(step):
        _, yy, xx = place(step)
        return [
            copy(kv.at[c, yy, xx], kv.at[c, yy, xx], s_ckv.at[step], r_ckv.at[step], c_peer),
            copy(info.at[c, yy, xx], info.at[c, yy, xx], s_cinf.at[step], r_cinf.at[step], c_peer),
        ]

    forward = []
    for i in range(nx - 1):
        xx = (x + i + 1) % nx
        blk = kv.at[c, y, xx, 0]
        forward.append(copy(blk, blk, s_fk.at[i], r_fk.at[i], y_peer))
        blk = info.at[c, y, xx]
        forward.append(copy(blk, blk, s_finf.at[i], r_finf.at[i], y_peer))
        blk = kv.at[c, 1 - y, x, 1]
        forward.append(copy(blk, blk, s_fv.at[i], r_fv.at[i], x_peers[i]))

    for one in direct + to_core(0):
        one.start()

    row_ids = lax.broadcasted_iota(jnp.int32, (rows, lanes), 0)

    def widen(row):
        return jnp.concatenate([row] * (lanes // 128), axis=1) if lanes > 128 else row

    def look(step, carry):
        @pl.when(step == 1)
        def _():
            for one in direct:
                one.wait_recv()
            for one in forward:
                one.start()
            for s in [*range(1, nx), nx]:
                for one in to_core(s):
                    one.start()

        @pl.when(step == nx + 1)
        def _():
            for one in forward:
                one.wait_recv()
            for s in range(nx + 1, half):
                for one in to_core(s):
                    one.start()

        @pl.when(step >= half)
        def _():
            for one in to_core(step - half):
                one.wait_recv()

        cc, yy, xx = place(step)
        raw = dot(kv[cc, yy, xx, 0], qs[...], 1, 1)
        dprobs = dot(kv[cc, yy, xx, 1], gs[...], 1, 1)
        high = top[...]
        old = high
        for b in range(na):
            first = info[cc, yy, xx, b * fields]
            upper = pos_q - widen(first)
            lower = jnp.zeros((1, lanes), jnp.int32)
            for d in range(docs):
                lower = lower + jnp.where(doc_q > d, widen(info[cc, yy, xx, b * fields + 1 + d]), 0)
            seen = (row_ids >= lower) & (row_ids <= upper)
            part = jnp.where(seen, raw[b * rows : (b + 1) * rows, :] * scale, NEG_BIG)
            sbuf[step, b * rows : (b + 1) * rows, :] = part
            high = jnp.maximum(high, jnp.max(part, axis=0, keepdims=True))
        dpbuf[step] = dprobs
        fade = jnp.exp2(old - high)
        weights = jnp.exp2(sbuf[step] - high)
        top[...] = high
        den[...] = den[...] * fade + jnp.sum(weights, axis=0, keepdims=True)
        cross[...] = cross[...] * fade + jnp.sum(weights * dprobs, axis=0, keepdims=True)
        return carry

    lax.fori_loop(0, CORES * half, look, 0)

    log_total = top[...] + jnp.log2(den[...])
    row_dot = cross[...] / den[...]

    def grads(step):
        cc, yy, xx = place(step)
        probs = jnp.exp2(sbuf[step] - log_total)
        dscores = (probs * (dpbuf[step] - row_dot)).astype(BF16)
        dqt[...] += dot(kv[cc, yy, xx, 0], dscores, 0, 0)
        return dot(dscores, qs[...], 1, 0) * inv_root, dot(probs.astype(BF16), gs[...], 1, 0)

    def core_copy(slot):
        return copy(core_out.at[slot], core_in.at[slot], s_rc.at[slot], r_rc.at[slot], c_peer)

    def other_core(i, carry):
        slot = half - 1 - i
        dk, dv = grads(half + slot)
        core_out[slot, 0] = dk.astype(BF16)
        core_out[slot, 1] = dv.astype(BF16)
        core_copy(slot).start()
        return carry

    lax.fori_loop(0, half, other_core, 0)

    def k1_copy(r):
        return copy(yk_out.at[r], yk_in.at[r], s_k1.at[r], r_k1.at[r], y_peer)

    def v1_copy(side, i):
        at = side * (nx - 1) + i
        return copy(xv_out.at[at], xv_in.at[at], s_v1.at[at], r_v1.at[at], x_peers[i])

    def this_core(i, carry):
        slot = half - 1 - i
        side, r = slot // nx, slot % nx
        dk, dv = grads(slot)
        core_copy(slot).wait_recv()
        dk = dk + core_in[slot, 0].astype(F32)
        dv = dv + core_in[slot, 1].astype(F32)

        @pl.when(side == 1)
        def _():
            yk_out[r] = dk.astype(BF16)
            k1_copy(r).start()

        @pl.when(side == 0)
        def _():
            acck[r] = dk

        @pl.when(r == 0)
        def _():
            accv[side] = dv

        for j in range(nx - 1):
            @pl.when(r == j + 1)
            def _():
                xv_out[side * (nx - 1) + j] = dv.astype(BF16)
                v1_copy(side, j).start()

        return carry

    lax.fori_loop(0, half, this_core, 0)

    def k2_copy(i):
        return copy(xk_out.at[i], xk_in.at[i], s_k2.at[i], r_k2.at[i], x_peers[i])

    v2 = copy(yv_out, yv_in, s_v2, r_v2, y_peer)
    for i in range(nx - 1):
        k1_copy(i + 1).wait_recv()
        xk_out[i] = (acck[i + 1] + yk_in[i + 1].astype(F32)).astype(BF16)
        k2_copy(i).start()
    total = accv[1]
    for i in range(nx - 1):
        v1_copy(1, i).wait_recv()
        total = total + xv_in[(nx - 1) + i].astype(F32)
    yv_out[...] = total.astype(BF16)
    v2.start()

    dq = jnp.transpose(dqt[...]) * inv_root
    for h in range(heads):
        dq_ref[:, h * 128 : (h + 1) * 128] = dq[h * rows : (h + 1) * rows, :]

    k1_copy(0).wait_recv()
    total_k = acck[0] + yk_in[0].astype(F32)
    total_v = accv[0]
    for i in range(nx - 1):
        v1_copy(0, i).wait_recv()
        total_v = total_v + xv_in[i].astype(F32)
    for i in range(nx - 1):
        k2_copy(i).wait_recv()
        total_k = total_k + xk_in[i].astype(F32)
    v2.wait_recv()
    total_v = total_v + yv_in[...].astype(F32)
    a_own[0] = total_k
    a_own[1] = total_v
    a_out[0] = total_k.astype(BF16)
    a_out[1] = total_v.astype(BF16)

    def ra_copy(i):
        there = pl.ds(pl.multiple_of(((a + i + 1) % na) * rows, rows), rows)
        return copy(a_out.at[:, there, :], a_in.at[i], s_ra.at[i], r_ra.at[i], a_peers[i])

    for i in range(na - 1):
        ra_copy(i).start()
    out_k = a_own[0, own_rows, :]
    out_v = a_own[1, own_rows, :]
    for i in range(na - 1):
        ra_copy(i).wait_recv()
        out_k = out_k + a_in[i, 0].astype(F32)
        out_v = out_v + a_in[i, 1].astype(F32)
    dk_ref[...] = out_k
    dv_ref[...] = out_v

    for one in gather + direct + forward + [v2]:
        one.wait_send()
    for s in range(half):
        for one in to_core(s):
            one.wait_send()
        core_copy(s).wait_send()
    for r in range(nx):
        k1_copy(r).wait_send()
    for i in range(nx - 1):
        v1_copy(0, i).wait_send()
        v1_copy(1, i).wait_send()
        k2_copy(i).wait_send()
    for i in range(na - 1):
        ra_copy(i).wait_send()


def on_device(queries, key_vecs, value_vecs, out_grad, positions, documents):
    nx = lax.axis_size("head")
    na = lax.axis_size("ctx") // (CORES * SIDES)
    rows, width = queries.shape
    heads = width // 128
    seq = rows * nx * na * CORES * SIDES
    docs = max(2, seq // 1024)
    chunk, lanes, half = na * rows, heads * rows, SIDES * nx
    cfg = (nx, na, rows, heads, docs)
    dma = pltpu.SemaphoreType.DMA
    near = max(nx - 1, 1)
    far = max(na - 1, 1)
    pair = lambda shape: [dma(shape), dma(shape)]
    vmem = pltpu.VMEM
    scratch = [
        vmem((lanes, 128), BF16),
        vmem((lanes, 128), BF16),
        vmem((CORES, SIDES, nx, 2, chunk, 128), BF16),
        vmem((CORES, SIDES, nx, na * (docs + 1), 1, 128), jnp.int32),
        vmem((CORES * half, chunk, lanes), F32),
        vmem((CORES * half, chunk, lanes), F32),
        vmem((1, lanes), F32),
        vmem((1, lanes), F32),
        vmem((1, lanes), F32),
        vmem((128, lanes), F32),
        vmem((nx, chunk, 128), F32),
        vmem((SIDES, chunk, 128), F32),
        vmem((half, 2, chunk, 128), BF16),
        vmem((half, 2, chunk, 128), BF16),
        vmem((nx, chunk, 128), BF16),
        vmem((nx, chunk, 128), BF16),
        vmem((SIDES * near, chunk, 128), BF16),
        vmem((SIDES * near, chunk, 128), BF16),
        vmem((near, chunk, 128), BF16),
        vmem((near, chunk, 128), BF16),
        vmem((chunk, 128), BF16),
        vmem((chunk, 128), BF16),
        vmem((2, chunk, 128), BF16),
        vmem((far, 2, rows, 128), BF16),
        vmem((2, chunk, 128), F32),
        *pair((far,)), *pair((far,)),
        *pair((near,)), *pair((near,)),
        *pair(()), *pair(()),
        *pair((near,)), *pair((near,)), *pair((near,)),
        *pair((half,)), *pair((half,)),
        *pair((half,)),
        *pair((nx,)), *pair((SIDES * near,)), *pair((near,)), *pair(()),
        *pair((far,)),
    ]
    whole = pl.BlockSpec(memory_space=pltpu.VMEM)
    pairs = lanes * seq
    return pl.pallas_call(
        functools.partial(kernel, cfg),
        out_shape=(
            jax.ShapeDtypeStruct((rows, width), F32),
            jax.ShapeDtypeStruct((rows, 128), F32),
            jax.ShapeDtypeStruct((rows, 128), F32),
        ),
        in_specs=[whole] * 6,
        out_specs=(whole, whole, whole),
        scratch_shapes=scratch,
        compiler_params=pltpu.CompilerParams(
            collective_id=0, has_side_effects=True, vmem_limit_bytes=48 * 1024 * 1024
        ),
        cost_estimate=pl.CostEstimate(
            flops=10 * pairs * 128, bytes_accessed=rows * width * 8, transcendentals=2 * pairs
        ),
    )(queries, key_vecs, value_vecs, out_grad, positions.reshape(1, rows), documents.reshape(1, rows))


def solution(mesh):
    tokens = P(("head", "ctx"), None)
    ids = P(("head", "ctx"))
    return jax.shard_map(
        on_device,
        mesh=mesh,
        in_specs=(tokens, tokens, tokens, tokens, ids, ids),
        out_specs=(tokens, tokens, tokens),
        check_vma=False,
    )
```

time: 322 us -> 41.5 us (0.13)
  waiting for transfers between devices: 149 us -> 0 us
  blocking collectives: 92.2 us -> 0 us
  Pallas kernels: 0 us -> 34.7 us
  starting transfers between devices: 27.5 us -> 0 us
  matrix products: 18.7 us -> 0 us
  between operations: 14.2 us -> 0.66 us
  local copies, waits for them, and re-layouts: 14 us -> 5.83 us
  other arithmetic: 3.74 us -> 0 us
    ppermute x76 -> x0, waiting for transfers between devices: 141 us -> none  [from_behind(): return lax.ppermute(block, axis, route)]
    all_gather x4 -> x0, blocking collectives: 50.4 us -> none  [the longest x1 22.2 us: on_device(): key_rows = lax.all_gather(key_own, 'ctx', axis=0, tiled=True)]
    unnamed x1 -> x0, blocking collectives: 41.8 us -> none
    pallas_call x0 -> x1, Pallas kernels: none -> 34.7 us  [on_device(): pl.pallas_call(functools.partial(kernel, cfg), out_shape=(jax.ShapeDtypeS...]
    dot_general x82 -> x0, matrix products: 18.7 us -> none  [the longest x17 4.96 us: masked_scores(): jnp.einsum('thd,kd->thk', query_cube, key_rows, preferred_element_type=jn...]
    ppermute x76 -> x0, starting transfers between devices: 16.4 us -> none  [from_behind(): return lax.ppermute(block, axis, route)]
    all_to_all x3 -> x0, starting transfers between devices: 11 us -> none  [the longest x1 4.21 us: on_device(): lax.all_to_all(queries, 'head', split_axis=1, concat_axis=0, tiled=True)]
    all_to_all x3 -> x0, waiting for transfers between devices: 7.75 us -> none  [the longest x1 4.03 us: on_device(): lax.all_to_all(out_grad, 'head', split_axis=1, concat_axis=0, tiled=True)]
  transfers between devices with their start and end apart: 80 -> 0, of which waited for: 33 -> 0; matrix products, arithmetic and copies ran while one was open for 9% -> 0% of each run, Pallas kernels for 0% -> 0%
where the time goes in v1:
time: 41.5 us; the launch traced here: 41.2 us
  Pallas kernels  34.7 us (84%)
  local copies, waits for them, and re-layouts  5.83 us (14%)
  between operations  0.66 us (2%)
    pallas_call x1, Pallas kernels, on_device(): pl.pallas_call(functools.partial(kernel, cfg), out_shape=(jax.ShapeDtypeS...  34.7 us
    unnamed x15, local copies, waits for them, and re-layouts  5.83 us

profile of v1, /device:TPU:0, one launch (start us, length us, event | category | flops | bytes accessed | tf_op | source)
XLA Modules:
  0.0 41.2 jit_solution(14159422553426923624)
XLA Ops:
  0.6 0.0 copy-start.4
  0.6 0.0 copy-start.5
  0.7 0.6 %copy-done.4 = s32[64]{0:T(128)S(1)} copy-done((s32[64]{0:T(128)S(1)}, s32[64]{0:T(128)}, u32[]{:S(2)}) %copy-start.4) | copy-done | bytes 280
  1.3 0.0 copy-done.5
  1.3 0.0 copy-start
  1.3 0.9 %copy-done = bf16[64,1024]{1,0:T(8,128)(2,1)S(1)} copy-done((bf16[64,1024]{1,0:T(8,128)(2,1)S(1)}, bf16[64,1024]{1,0:T(8,128)(2,1)}, u32[]{:S(2)}) %copy-start) | copy-done | bytes 131096
  2.2 0.0 copy-start.1
  2.2 0.9 %copy-done.1 = bf16[64,1024]{1,0:T(8,128)(2,1)S(1)} copy-done((bf16[64,1024]{1,0:T(8,128)(2,1)S(1)}, bf16[64,1024]{1,0:T(8,128)(2,1)}, u32[]{:S(2)}) %copy-start.1) | copy-done | bytes 131096
  3.1 0.0 copy-start.2
  3.1 0.7 %copy-done.2 = bf16[64,128]{1,0:T(8,128)(2,1)S(1)} copy-done((bf16[64,128]{1,0:T(8,128)(2,1)S(1)}, bf16[64,128]{1,0:T(8,128)(2,1)}, u32[]{:S(2)}) %copy-start.2) | copy-done | bytes 16408
  3.8 0.0 copy-start.3
  3.8 0.7 %copy-done.3 = bf16[64,128]{1,0:T(8,128)(2,1)S(1)} copy-done((bf16[64,128]{1,0:T(8,128)(2,1)S(1)}, bf16[64,128]{1,0:T(8,128)(2,1)}, u32[]{:S(2)}) %copy-start.3) | copy-done | bytes 16408
  4.5 34.7 %shard_map.85 = (f32[64,1024]{1,0:T(8,128)S(1)}, f32[64,128]{1,0:T(8,128)S(1)}, f32[64,128]{1,0:T(8,128)S(1)}) custom-call(bf16[64,1024]{1,0:T(8,128)(2,1)S(1)} %copy-done, bf16[64,128]{1,0:T(8,128)(2,1)S(1)} %copy-done.2, bf16[64,128]{1,0:T(8,128)(2,1)S(1)} %copy-done.3, bf16[64,1024]{1,0:T(8,128)(2,1)S(1)} %copy-done.1, s32[1,64]{1,0:T(1,128)S(1)} %bitcast.2, ...), custom_call_target="tpu_custom_call" | custom-call | flops 1342177280 | bytes 524288 | tf_op jit(solution)/shard_map/pallas_call | solution.py:371
  39.2 0.7 %copy.12 = f32[64,1024]{1,0:T(8,128)} copy(f32[64,1024]{1,0:T(8,128)S(1)} %get-tuple-element.6) | data formatting | bytes 524288
  39.9 0.6 %copy.13 = f32[64,128]{1,0:T(8,128)} copy(f32[64,128]{1,0:T(8,128)S(1)} %get-tuple-element.7) | data formatting | bytes 65536
  40.6 0.6 %copy.14 = f32[64,128]{1,0:T(8,128)} copy(f32[64,128]{1,0:T(8,128)S(1)} %get-tuple-element.8) | data formatting | bytes 65536
Async XLA Ops:
  0.6 0.7 %copy-start.4 = (s32[64]{0:T(128)S(1)}, s32[64]{0:T(128)}, u32[]{:S(2)}) copy-start(s32[64]{0:T(128)} %param.10) | copy-start | bytes 772
  0.6 0.7 %copy-start.5 = (s32[64]{0:T(128)S(1)}, s32[64]{0:T(128)}, u32[]{:S(2)}) copy-start(s32[64]{0:T(128)} %param.11) | copy-start | bytes 772
  1.3 0.9 %copy-start = (bf16[64,1024]{1,0:T(8,128)(2,1)S(1)}, bf16[64,1024]{1,0:T(8,128)(2,1)}, u32[]{:S(2)}) copy-start(bf16[64,1024]{1,0:T(8,128)(2,1)} %q_ref.1) | copy-start | bytes 393220
  2.2 0.9 %copy-start.1 = (bf16[64,1024]{1,0:T(8,128)(2,1)S(1)}, bf16[64,1024]{1,0:T(8,128)(2,1)}, u32[]{:S(2)}) copy-start(bf16[64,1024]{1,0:T(8,128)(2,1)} %g_ref.1) | copy-start | bytes 393220
  3.1 0.7 %copy-start.2 = (bf16[64,128]{1,0:T(8,128)(2,1)S(1)}, bf16[64,128]{1,0:T(8,128)(2,1)}, u32[]{:S(2)}) copy-start(bf16[64,128]{1,0:T(8,128)(2,1)} %k_ref.1) | copy-start | bytes 49156
  3.8 0.7 %copy-start.3 = (bf16[64,128]{1,0:T(8,128)(2,1)S(1)}, bf16[64,128]{1,0:T(8,128)(2,1)}, u32[]{:S(2)}) copy-start(bf16[64,128]{1,0:T(8,128)(2,1)} %v_ref.1) | copy-start | bytes 49156

commit v2 on v1

v2 whole, which is shorter than its diff:
```python
import functools
import math

import jax
import jax.numpy as jnp
from jax import lax
from jax.experimental import pallas as pl
from jax.experimental.pallas import tpu as pltpu
from jax.sharding import PartitionSpec as P

MESH = pl.DeviceIdType.MESH
NEG_BIG = -1e30
CORES = 2
SIDES = 2
F32 = jnp.float32
BF16 = jnp.bfloat16


def dot(lhs, rhs, lhs_dim, rhs_dim):
    return lax.dot_general(
        lhs, rhs, (((lhs_dim,), (rhs_dim,)), ((), ())), preferred_element_type=F32
    )


def xor(left, right, bits):
    total = 0
    for b in range(bits):
        total = total + ((left // 2**b + right // 2**b) % 2) * 2**b
    return total


def kernel(
    cfg,
    q_ref, k_ref, v_ref, g_ref, pos_ref, doc_ref,
    dq_ref, dk_ref, dv_ref,
    raw, qs, gs, kv, info, ids, sbuf, dpbuf, stats, dqt, dq_in, acck, accv,
    yk_out, yk_in, xv_out, xv_in, xk_out, xk_in, yv_out, yv_in, a_out, a_in, a_own,
    *sems,
):
    nx, na, rows, heads, docs, names = cfg
    sem = dict(zip(names, sems))
    lanes = heads * rows
    half = SIDES * nx
    x_bits, a_bits = (nx - 1).bit_length(), (na - 1).bit_length()
    inv_root = 1.0 / math.sqrt(128)
    scale = inv_root * math.log2(math.e)

    x = lax.axis_index("head")
    ctx = lax.axis_index("ctx")
    a, y, c = ctx // 4, (ctx // 2) % 2, ctx % 2

    def a_peer(r):
        return (x, xor(a, r, a_bits) * 4 + y * 2 + c)

    def x_peer(r):
        return (xor(x, r, x_bits), ctx)

    y_peer = (x, a * 4 + (1 - y) * 2 + c)
    c_peer = (x, a * 4 + y * 2 + 1 - c)

    def copy(src, dst, name, at, to):
        send, recv = sem["s_" + name], sem["r_" + name]
        return pltpu.make_async_remote_copy(
            src_ref=src, dst_ref=dst, send_sem=send.at[at], recv_sem=recv.at[at], device_id=to, device_id_type=MESH
        )

    barrier = pltpu.get_barrier_semaphore()
    everyone = [a_peer(r) for r in range(1, na)] + [x_peer(r) for r in range(1, nx)] + [y_peer, c_peer]
    for to in everyone:
        pl.semaphore_signal(barrier, inc=1, device_id=to, device_id_type=MESH)

    def rows_of(block):
        return pl.ds(pl.multiple_of(block * rows, rows), rows)

    own_rows = rows_of(a)
    own = [
        pltpu.make_async_copy(src, dst, sem["own"].at[i])
        for i, (src, dst) in enumerate([
            (pos_ref, ids.at[0]), (doc_ref, ids.at[1]),
            (k_ref, kv.at[y, x, 0, own_rows, :]), (v_ref, kv.at[y, x, 1, own_rows, :]),
            (q_ref, raw.at[0, c]), (g_ref, raw.at[1, c]),
        ])
    ]
    for one in own:
        one.start()

    pl.semaphore_wait(barrier, len(everyone))

    k_slot, v_slot = kv.at[y, x, 0, own_rows, :], kv.at[y, x, 1, own_rows, :]
    first = []
    for r in range(1, na):
        first.append(copy(k_ref, k_slot, "ak", r, a_peer(r)))
        first.append(copy(v_ref, v_slot, "av", r, a_peer(r)))
    first.append(copy(k_ref, k_slot, "y0k", 0, y_peer))
    first.append(copy(v_ref, v_slot, "y0v", 0, y_peer))
    for r in range(1, nx):
        first.append(copy(k_ref, k_slot, "x0k", r, x_peer(r)))
        first.append(copy(v_ref, v_slot, "x0v", r, x_peer(r)))
    for one in first:
        one.start()

    share = [copy(q_ref, raw.at[0, c], "qg", 0, c_peer), copy(g_ref, raw.at[1, c], "qg", 1, c_peer)]
    for one in share:
        one.start()

    fields = docs + 1
    own_info = a * fields
    own[0].wait()
    own[1].wait()
    pos_own = ids[0]
    doc_own = ids[1]
    info[y, x, own_info] = jnp.broadcast_to(pos_own[:, 0:1], (1, 128))
    for d in range(docs):
        tally = jnp.sum(jnp.where(doc_own == d, 1, 0), axis=1, keepdims=True)
        info[y, x, own_info + 1 + d] = jnp.broadcast_to(tally, (1, 128))
    info_slot = info.at[y, x, pl.ds(own_info, fields)]
    facts = [copy(info_slot, info_slot, "ainf", r, a_peer(r)) for r in range(1, na)]
    spare = 128 - 2 * rows
    pieces = [pos_own, doc_own] + ([jnp.zeros((1, spare), jnp.int32)] if spare else [])
    info_q = sem["info_q"]
    info_q[c] = jnp.concatenate(pieces, axis=1)
    facts.append(copy(info_q.at[c], info_q.at[c], "idq", 0, c_peer))
    for one in facts:
        one.start()

    def block_copies(step):
        block = kv.at[y, x, :, rows_of(xor(a, step, a_bits)), :]
        return [copy(block, block, "x", step * nx + r, x_peer(r)) for r in range(1, nx)] + [
            copy(block, block, "y", step, y_peer)
        ]

    def forwards(step):
        at = rows_of(xor(a, step, a_bits))
        found = []
        for r in range(1, nx):
            key_block = kv.at[y, xor(x, r, x_bits), 0, at, :]
            found.append(copy(key_block, key_block, "fk", step * nx + r, y_peer))
            value_block = kv.at[1 - y, x, 1, at, :]
            found.append(copy(value_block, value_block, "fv", step * nx + r, x_peer(r)))
        return found

    def a_arrived(step):
        block = kv.at[y, x, 0, own_rows, :]
        copy(block, block, "ak", step, a_peer(1)).wait_recv()
        copy(block, block, "av", step, a_peer(1)).wait_recv()

    def send_all(copies):
        for one in copies:
            one.start()

    def relay(step, carry):
        a_arrived(step)
        send_all(block_copies(step))

        @pl.when(step == 1)
        def _():
            for one in first[2 * (na - 1):]:
                one.wait_recv()

        @pl.when(step > 1)
        def _():
            for one in block_copies(step - 1):
                one.wait_recv()

        send_all(forwards(step - 1))
        return carry

    lax.fori_loop(1, na, relay, 0)

    for one in facts:
        one.wait_recv()
    mine_info = info.at[y, x]
    facts_xy = [copy(mine_info, mine_info, "xinf", r, x_peer(r)) for r in range(1, nx)]
    facts_xy.append(copy(mine_info, mine_info, "yinf", 0, y_peer))
    send_all(facts_xy)

    for one in own[2:]:
        one.wait()
    for one in share:
        one.wait_recv()
    for k in range(CORES):
        for h in range(heads):
            at = k * lanes + h * rows
            qs[at : at + rows, :] = raw[0, k, :, h * 128 : (h + 1) * 128]
            gs[at : at + rows, :] = raw[1, k, :, h * 128 : (h + 1) * 128]
    both = [info_q[k] for k in range(CORES)]
    pos_q = jnp.concatenate([one[:, :rows] for one in both for _ in range(heads)], axis=1)
    doc_q = jnp.concatenate([one[:, rows : 2 * rows] for one in both for _ in range(heads)], axis=1)
    wide = CORES * lanes
    stats[0] = jnp.full((1, wide), NEG_BIG, F32)
    stats[1] = jnp.zeros((1, wide), F32)
    stats[2] = jnp.zeros((1, wide), F32)
    dqt[...] = jnp.zeros(dqt.shape, F32)

    def place(step):
        return ((y + step // nx) % SIDES, xor(x, step % nx, x_bits))

    facts_fwd = []
    for r in range(1, nx):
        blk = info.at[y, xor(x, r, x_bits)]
        facts_fwd.append(copy(blk, blk, "finf", r, y_peer))

    row_ids = lax.broadcasted_iota(jnp.int32, (rows, wide), 0)

    def widen(row):
        return jnp.concatenate([row] * (wide // 128), axis=1)

    def look(step, carry):
        @pl.when(step == 1)
        def _():
            for one in block_copies(na - 1):
                one.wait_recv()
            send_all(forwards(na - 1))
            for one in facts_xy:
                one.wait_recv()
            send_all(facts_fwd)

        @pl.when(step == nx + 1)
        def _():
            for one in facts_fwd:
                one.wait_recv()
            for s in range(na):
                for one in forwards(s):
                    one.wait_recv()

        yy, xx = place(step)
        scores = dot(kv[yy, xx, 0], qs[...], 1, 1)
        dprobs = dot(kv[yy, xx, 1], gs[...], 1, 1)
        old = stats[0]
        high = old
        for b in range(na):
            upper = pos_q - widen(info[yy, xx, b * fields])
            lower = jnp.zeros((1, wide), jnp.int32)
            for d in range(docs):
                lower = lower + jnp.where(doc_q > d, widen(info[yy, xx, b * fields + 1 + d]), 0)
            seen = (row_ids >= lower) & (row_ids <= upper)
            part = jnp.where(seen, scores[b * rows : (b + 1) * rows, :] * scale, NEG_BIG)
            sbuf[step, b * rows : (b + 1) * rows, :] = part
            high = jnp.maximum(high, jnp.max(part, axis=0, keepdims=True))
        dpbuf[step] = dprobs
        fade = jnp.exp2(old - high)
        weights = jnp.exp2(sbuf[step] - high)
        stats[0] = high
        stats[1] = stats[1] * fade + jnp.sum(weights, axis=0, keepdims=True)
        stats[2] = stats[2] * fade + jnp.sum(weights * dprobs, axis=0, keepdims=True)
        return carry

    lax.fori_loop(0, half, look, 0)

    stats_in = sem["stats_in"]
    swap = copy(stats, stats_in, "stat", 0, c_peer)
    swap.start()
    swap.wait_recv()
    high = jnp.maximum(stats[0], stats_in[0])
    here, there = jnp.exp2(stats[0] - high), jnp.exp2(stats_in[0] - high)
    denom = stats[1] * here + stats_in[1] * there
    log_total = high + jnp.log2(denom)
    row_dot = (stats[2] * here + stats_in[2] * there) / denom

    def k1_copy(r):
        return copy(yk_out.at[r], yk_in.at[r], "k1", r, y_peer)

    def v1_copy(side, r):
        at = side * nx + r
        return copy(xv_out.at[at], xv_in.at[at], "v1", at, x_peer(r))

    def grads(i, carry):
        step = half - 1 - i
        side, r = step // nx, step % nx
        yy, xx = place(step)
        probs = jnp.exp2(sbuf[step] - log_total)
        dscores = (probs * (dpbuf[step] - row_dot)).astype(BF16)
        dk = dot(dscores, qs[...], 1, 0) * inv_root
        dv = dot(probs.astype(BF16), gs[...], 1, 0)

        @pl.when(side == 1)
        def _():
            yk_out[r] = dk.astype(BF16)
            k1_copy(r).start()

        @pl.when(side == 0)
        def _():
            acck[r] = dk

        @pl.when(r == 0)
        def _():
            accv[side] = dv

        @pl.when(r > 0)
        def _():
            xv_out[side * nx + r] = dv.astype(BF16)
            v1_copy(side, r).start()

        part = dot(kv[yy, xx, 0], dscores, 0, 0)
        for k in range(CORES):
            dqt[k] += part[:, k * lanes : (k + 1) * lanes]
        return carry

    lax.fori_loop(0, half, grads, 0)

    def k2_copy(r):
        return copy(xk_out.at[r], xk_in.at[r], "k2", r, x_peer(r))

    v2 = copy(yv_out, yv_in, "v2", 0, y_peer)
    swap_dq = copy(dqt.at[1 - c], dq_in, "dq", 0, c_peer)
    for r in range(1, nx):
        k1_copy(r).wait_recv()
        xk_out[r] = (acck[r] + yk_in[r].astype(F32)).astype(BF16)
        k2_copy(r).start()
    total = accv[1]
    for r in range(1, nx):
        v1_copy(1, r).wait_recv()
        total = total + xv_in[nx + r].astype(F32)
    yv_out[...] = total.astype(BF16)
    v2.start()
    swap_dq.start()

    k1_copy(0).wait_recv()
    total_k = acck[0] + yk_in[0].astype(F32)
    a_own[0] = total_k
    total_v = accv[0]
    for r in range(1, nx):
        v1_copy(0, r).wait_recv()
        total_v = total_v + xv_in[r].astype(F32)
    a_own[1] = total_v

    dq_own = sem["dq_own"]
    swap_dq.wait_recv()
    dq = jnp.transpose(dqt[c] + dq_in[...]) * inv_root
    for h in range(heads):
        dq_own[:, h * 128 : (h + 1) * 128] = dq[h * rows : (h + 1) * rows, :]
    results = [
        pltpu.make_async_copy(src, dst, sem["out"].at[i])
        for i, (src, dst) in enumerate([(dq_own, dq_ref), (sem["dk_own"], dk_ref), (sem["dv_own"], dv_ref)])
    ]
    results[0].start()

    def ra_copy(which, r):
        at = which * na + r
        src = a_out.at[which, rows_of(xor(a, r, a_bits)), :]
        return copy(src, a_in.at[at], "ra", at, a_peer(r))

    total_k = a_own[0]
    for r in range(1, nx):
        k2_copy(r).wait_recv()
        total_k = total_k + xk_in[r].astype(F32)
    a_out[0] = total_k.astype(BF16)
    a_own[0] = total_k
    for r in range(1, na):
        ra_copy(0, r).start()
    v2.wait_recv()
    total_v = a_own[1] + yv_in[...].astype(F32)
    a_out[1] = total_v.astype(BF16)
    a_own[1] = total_v
    for r in range(1, na):
        ra_copy(1, r).start()

    for one in first + share + facts + facts_xy + facts_fwd + [swap, v2, swap_dq]:
        one.wait_send()

    def sent(step, carry):
        @pl.when(step > 0)
        def _():
            for one in block_copies(step):
                one.wait_send()

        for one in forwards(step):
            one.wait_send()
        return carry

    lax.fori_loop(0, na, sent, 0)
    for r in range(nx):
        k1_copy(r).wait_send()
    for r in range(1, nx):
        v1_copy(0, r).wait_send()
        v1_copy(1, r).wait_send()
        k2_copy(r).wait_send()

    for which, out in ((0, sem["dk_own"]), (1, sem["dv_own"])):
        done = a_own[which, own_rows, :]
        for r in range(1, na):
            ra_copy(which, r).wait_recv()
            done = done + a_in[which * na + r].astype(F32)
        out[...] = done
        results[1 + which].start()
    for which in range(2):
        for r in range(1, na):
            ra_copy(which, r).wait_send()
    for one in results:
        one.wait()


def hand_over(*refs):
    count = (len(refs) - 1) // 2
    moves = [pltpu.make_async_copy(refs[i], refs[count + i], refs[-1].at[i]) for i in range(count)]
    for one in moves:
        one.start()
    for one in moves:
        one.wait()


def on_device(queries, key_vecs, value_vecs, out_grad, positions, documents):
    nx = lax.axis_size("head")
    na = lax.axis_size("ctx") // (CORES * SIDES)
    rows, width = queries.shape
    heads = width // 128
    seq = rows * nx * na * CORES * SIDES
    docs = max(2, seq // 1024)
    chunk, lanes, half = na * rows, heads * rows, SIDES * nx
    wide = CORES * lanes
    dma = pltpu.SemaphoreType.DMA
    vmem = pltpu.VMEM
    copies = {
        "ak": na, "av": na, "ainf": na, "idq": 1, "y0k": 1, "y0v": 1, "x0k": nx, "x0v": nx, "qg": 2,
        "x": na * nx, "y": na, "fk": na * nx, "fv": na * nx, "xinf": nx, "yinf": 1, "finf": nx, "stat": 1,
        "k1": nx, "v1": SIDES * nx, "k2": nx, "v2": 1, "dq": 1, "ra": 2 * na,
    }
    names, tail = [], []
    for name, count in copies.items():
        names += ["s_" + name, "r_" + name]
        tail += [dma((count,)), dma((count,))]
    names += ["own", "out", "info_q", "stats_in", "dq_own", "dk_own", "dv_own"]
    tail += [dma((6,)), dma((3,)), vmem((CORES, 1, 128), jnp.int32), vmem((3, 1, wide), F32)]
    tail += [vmem((rows, width), F32), vmem((rows, 128), F32), vmem((rows, 128), F32)]
    scratch = [
        vmem((2, CORES, rows, width), BF16),
        vmem((wide, 128), BF16),
        vmem((wide, 128), BF16),
        vmem((SIDES, nx, 2, chunk, 128), BF16),
        vmem((SIDES, nx, na * (docs + 1), 1, 128), jnp.int32),
        vmem((2, 1, rows), jnp.int32),
        vmem((half, chunk, wide), F32),
        vmem((half, chunk, wide), F32),
        vmem((3, 1, wide), F32),
        vmem((CORES, 128, lanes), F32),
        vmem((128, lanes), F32),
        vmem((nx, chunk, 128), F32),
        vmem((SIDES, chunk, 128), F32),
        vmem((nx, chunk, 128), BF16),
        vmem((nx, chunk, 128), BF16),
        vmem((SIDES * nx, chunk, 128), BF16),
        vmem((SIDES * nx, chunk, 128), BF16),
        vmem((nx, chunk, 128), BF16),
        vmem((nx, chunk, 128), BF16),
        vmem((chunk, 128), BF16),
        vmem((chunk, 128), BF16),
        vmem((2, chunk, 128), BF16),
        vmem((2 * na, rows, 128), BF16),
        vmem((2, chunk, 128), F32),
    ] + tail
    cfg = (nx, na, rows, heads, docs, names)
    far = pl.BlockSpec(memory_space=pltpu.HBM)
    pairs = lanes * seq
    shapes = (
        jax.ShapeDtypeStruct((rows, width), F32),
        jax.ShapeDtypeStruct((rows, 128), F32),
        jax.ShapeDtypeStruct((rows, 128), F32),
    )
    found = pl.pallas_call(
        functools.partial(kernel, cfg),
        out_shape=shapes,
        in_specs=[far] * 6,
        out_specs=(far, far, far),
        scratch_shapes=scratch,
        compiler_params=pltpu.CompilerParams(
            collective_id=0, has_side_effects=True, vmem_limit_bytes=64 * 1024 * 1024
        ),
        cost_estimate=pl.CostEstimate(
            flops=10 * pairs * 128, bytes_accessed=rows * width * 8, transcendentals=2 * pairs
        ),
    )(queries, key_vecs, value_vecs, out_grad, positions.reshape(1, rows), documents.reshape(1, rows))
    return pl.pallas_call(
        hand_over,
        out_shape=shapes,
        in_specs=[far] * 3,
        out_specs=(far, far, far),
        scratch_shapes=[dma((3,))],
        compiler_params=pltpu.CompilerParams(vmem_limit_bytes=64 * 1024 * 1024),
    )(*found)


def solution(mesh):
    tokens = P(("head", "ctx"), None)
    ids = P(("head", "ctx"))
    return jax.shard_map(
        on_device,
        mesh=mesh,
        in_specs=(tokens, tokens, tokens, tokens, ids, ids),
        out_specs=(tokens, tokens, tokens),
        check_vma=False,
    )
```

time: 41.5 us -> 45.3 us (1.092)
  Pallas kernels: 34.7 us -> 44.5 us
  local copies, waits for them, and re-layouts: 5.83 us -> 0 us
    pallas_call x1 -> x2, Pallas kernels: 34.7 us -> 44.5 us  [the longest x1 33.4 us: on_device(): pl.pallas_call(functools.partial(kernel, cfg), out_shape=shapes, in_specs...]
    unnamed x15 -> x0, local copies, waits for them, and re-layouts: 5.83 us -> none
where the time goes in v2:
time: 45.3 us; the launch traced here: 45.1 us
  Pallas kernels  44.5 us (98%)
  between operations  0.64 us (1%)
    pallas_call x1, Pallas kernels, on_device(): pl.pallas_call(functools.partial(kernel, cfg), out_shape=shapes, in_specs...  33.4 us
    pallas_call x1, Pallas kernels, on_device(): pl.pallas_call(hand_over, out_shape=shapes, in_specs=[far] * 3, out_specs...  11.1 us

profile of v2, /device:TPU:0, one launch (start us, length us, event | category | flops | bytes accessed | tf_op | source)
XLA Modules:
  0.0 45.1 jit_solution(11851882669701951071)
XLA Ops:
  0.6 33.4 %shard_map.85 = (f32[64,1024]{1,0:T(8,128)}, f32[64,128]{1,0:T(8,128)}, f32[64,128]{1,0:T(8,128)}) custom-call(bf16[64,1024]{1,0:T(8,128)(2,1)} %q_ref.1, bf16[64,128]{1,0:T(8,128)(2,1)} %k_ref.1, bf16[64,128]{1,0:T(8,128)(2,1)} %v_ref.1, bf16[64,1024]{1,0:T(8,128)(2,1)} %g_ref.1, s32[1,64]{1,0:T(1,128)} %bitcast.2, s32[1,64]{1,0:T(1,128)} %bitcast.3), custom_call_target="tpu_custom_call" | custom-call | flops 1342177280 | bytes 524288 | tf_op jit(solution)/shard_map/pallas_call | solution.py:459
  34.1 11.1 %shard_map.86 = (f32[64,1024]{1,0:T(8,128)}, f32[64,128]{1,0:T(8,128)}, f32[64,128]{1,0:T(8,128)}) custom-call(f32[64,1024]{1,0:T(8,128)} %get-tuple-element.6.refs_0_, f32[64,128]{1,0:T(8,128)} %get-tuple-element.7.refs_1_, f32[64,128]{1,0:T(8,128)} %get-tuple-element.8.refs_2_), custom_call_target="tpu_custom_call" | custom-call | tf_op jit(solution)/shard_map/pallas_call | solution.py:472

commit v3 on v2

v3 whole, which is shorter than its diff:
```python
import functools
import math

import jax
import jax.numpy as jnp
from jax import lax
from jax.experimental import pallas as pl
from jax.experimental.pallas import tpu as pltpu
from jax.sharding import PartitionSpec as P

MESH = pl.DeviceIdType.MESH
NEG_BIG = -1e30
CORES = 2
LAG = 2
SIDES = 2
F32 = jnp.float32
BF16 = jnp.bfloat16


def dot(lhs, rhs, lhs_dim, rhs_dim):
    return lax.dot_general(
        lhs, rhs, (((lhs_dim,), (rhs_dim,)), ((), ())), preferred_element_type=F32
    )


def xor(left, right, bits):
    total = 0
    for b in range(bits):
        total = total + ((left // 2**b + right // 2**b) % 2) * 2**b
    return total


def kernel(
    cfg,
    q_ref, k_ref, v_ref, g_ref, pos_ref, doc_ref,
    dq_ref, dk_ref, dv_ref,
    raw, qs, gs, kv, info, ids, sbuf, dpbuf, stats, dqt, dq_in, acck, accv,
    k_out, yk_in, v_out, xv_in, xk_out, xk_in, yv_out, yv_in, a_out, a_in, a_own,
    *sems,
):
    nx, na, rows, heads, docs, names = cfg
    sem = dict(zip(names, sems))
    lanes = heads * rows
    group = SIDES * nx
    x_bits, a_bits = (nx - 1).bit_length(), (na - 1).bit_length()
    inv_root = 1.0 / math.sqrt(128)
    scale = inv_root * math.log2(math.e)

    x = lax.axis_index("head")
    ctx = lax.axis_index("ctx")
    a, y, c = ctx // 4, (ctx // 2) % 2, ctx % 2

    def a_peer(r):
        return (x, xor(a, r, a_bits) * 4 + y * 2 + c)

    def x_peer(r):
        return (xor(x, r, x_bits), ctx)

    y_peer = (x, a * 4 + (1 - y) * 2 + c)
    c_peer = (x, a * 4 + y * 2 + 1 - c)

    def copy(src, dst, name, at, to):
        send, recv = sem["s_" + name], sem["r_" + name]
        return pltpu.make_async_remote_copy(
            src_ref=src, dst_ref=dst, send_sem=send.at[at], recv_sem=recv.at[at], device_id=to, device_id_type=MESH
        )

    barrier = pltpu.get_barrier_semaphore()
    everyone = [a_peer(r) for r in range(1, na)] + [x_peer(r) for r in range(1, nx)] + [y_peer, c_peer]
    for to in everyone:
        pl.semaphore_signal(barrier, inc=1, device_id=to, device_id_type=MESH)

    k_slot, v_slot = kv.at[a, 0, y, x], kv.at[a, 1, y, x]
    own = [
        pltpu.make_async_copy(src, dst, sem["own"].at[i])
        for i, (src, dst) in enumerate([
            (pos_ref, ids.at[0]), (doc_ref, ids.at[1]),
            (k_ref, k_slot), (v_ref, v_slot),
            (q_ref, raw.at[0, c]), (g_ref, raw.at[1, c]),
        ])
    ]
    for one in own:
        one.start()

    pl.semaphore_wait(barrier, len(everyone))

    first = []
    for r in range(1, na):
        first.append(copy(k_ref, k_slot, "ak", r, a_peer(r)))
        first.append(copy(v_ref, v_slot, "av", r, a_peer(r)))
    first.append(copy(k_ref, k_slot, "y0k", 0, y_peer))
    first.append(copy(v_ref, v_slot, "y0v", 0, y_peer))
    for r in range(1, nx):
        first.append(copy(k_ref, k_slot, "x0k", r, x_peer(r)))
        first.append(copy(v_ref, v_slot, "x0v", r, x_peer(r)))
    for one in first:
        one.start()

    share = [copy(q_ref, raw.at[0, c], "qg", 0, c_peer), copy(g_ref, raw.at[1, c], "qg", 1, c_peer)]
    for one in share:
        one.start()

    fields = docs + 1
    own[0].wait()
    own[1].wait()
    pos_own = ids[0]
    doc_own = ids[1]
    info[a, y, x, 0] = jnp.broadcast_to(pos_own[:, 0:1], (1, 128))
    for d in range(docs):
        tally = jnp.sum(jnp.where(doc_own == d, 1, 0), axis=1, keepdims=True)
        info[a, y, x, 1 + d] = jnp.broadcast_to(tally, (1, 128))
    info_slot = info.at[a, y, x]
    facts_x = [copy(info_slot, info_slot, "xinf", r, x_peer(r)) for r in range(1, nx)]
    facts = facts_x + [copy(info_slot, info_slot, "yinf", 0, y_peer)]
    spare = 128 - 2 * rows
    pieces = [pos_own, doc_own] + ([jnp.zeros((1, spare), jnp.int32)] if spare else [])
    info_q = sem["info_q"]
    info_q[c] = jnp.concatenate(pieces, axis=1)
    id_share = copy(info_q.at[c], info_q.at[c], "idq", 0, c_peer)
    for one in facts + [id_share]:
        one.start()

    def block_copies(step):
        block = kv.at[xor(a, step, a_bits), :, y, x]
        return [copy(block, block, "x", step * nx + r, x_peer(r)) for r in range(1, nx)] + [
            copy(block, block, "y", step, y_peer)
        ]

    def forwards(step):
        at = xor(a, step, a_bits)
        found = []
        for r in range(1, nx):
            key_block = kv.at[at, 0, y, xor(x, r, x_bits)]
            found.append(copy(key_block, key_block, "fk", step * nx + r, y_peer))
            value_block = kv.at[at, 1, 1 - y, x]
            found.append(copy(value_block, value_block, "fv", step * nx + r, x_peer(r)))
        return found

    def a_arrived(step):
        block = k_slot
        copy(block, block, "ak", step, a_peer(1)).wait_recv()
        copy(block, block, "av", step, a_peer(1)).wait_recv()

    def send_all(copies):
        for one in copies:
            one.start()

    def relay(step, carry):
        a_arrived(step)
        send_all(block_copies(step))

        @pl.when(step == 1)
        def _():
            for one in first[2 * (na - 1):]:
                one.wait_recv()

        @pl.when(step > 1)
        def _():
            for one in block_copies(step - 1):
                one.wait_recv()

        send_all(forwards(step - 1))
        return carry

    facts_fwd = []
    for r in range(1, nx):
        blk = info.at[a, y, xor(x, r, x_bits)]
        facts_fwd.append(copy(blk, blk, "finf", r, y_peer))
    facts_a = [copy(info.at[a], info.at[a], "ainf", r, a_peer(r)) for r in range(1, na)]
    for one in facts_x:
        one.wait_recv()
    send_all(facts_fwd)
    for one in facts[nx - 1:] + facts_fwd:
        one.wait_recv()
    send_all(facts_a)

    lax.fori_loop(1, na, relay, 0)

    for one in own[2:]:
        one.wait()
    for one in share + [id_share]:
        one.wait_recv()
    for k in range(CORES):
        for h in range(heads):
            at = k * lanes + h * rows
            qs[at : at + rows, :] = raw[0, k, :, h * 128 : (h + 1) * 128]
            gs[at : at + rows, :] = raw[1, k, :, h * 128 : (h + 1) * 128]
    both = [info_q[k] for k in range(CORES)]
    pos_q = jnp.concatenate([one[:, :rows] for one in both for _ in range(heads)], axis=1)
    doc_q = jnp.concatenate([one[:, rows : 2 * rows] for one in both for _ in range(heads)], axis=1)
    wide = CORES * lanes
    stats[0] = jnp.full((1, wide), NEG_BIG, F32)
    stats[1] = jnp.zeros((1, wide), F32)
    stats[2] = jnp.zeros((1, wide), F32)
    dqt[...] = jnp.zeros(dqt.shape, F32)
    for one in facts_a:
        one.wait_recv()

    row_ids = lax.broadcasted_iota(jnp.int32, (rows, wide), 0)

    def widen(row):
        return jnp.concatenate([row] * (wide // 128), axis=1)

    def chunk_of(step, which):
        return kv[xor(a, step, a_bits), which].reshape(group * rows, 128)

    def look(step, carry):
        @pl.when(step == 1)
        def _():
            for one in block_copies(na - 1):
                one.wait_recv()
            send_all(forwards(na - 1))

        for one in forwards(step):
            one.wait_recv()

        scores = dot(chunk_of(step, 0), qs[...], 1, 1)
        dprobs = dot(chunk_of(step, 1), gs[...], 1, 1)
        old = stats[0]
        high = old
        at = xor(a, step, a_bits)
        for b in range(group):
            row = lambda f: widen(info[at, b // nx, b % nx, f])
            upper = pos_q - row(0)
            lower = jnp.zeros((1, wide), jnp.int32)
            for d in range(docs):
                lower = lower + jnp.where(doc_q > d, row(1 + d), 0)
            seen = (row_ids >= lower) & (row_ids <= upper)
            part = jnp.where(seen, scores[b * rows : (b + 1) * rows, :] * scale, NEG_BIG)
            sbuf[step, b * rows : (b + 1) * rows, :] = part
            high = jnp.maximum(high, jnp.max(part, axis=0, keepdims=True))
        dpbuf[step] = dprobs
        fade = jnp.exp2(old - high)
        weights = jnp.exp2(sbuf[step] - high)
        stats[0] = high
        stats[1] = stats[1] * fade + jnp.sum(weights, axis=0, keepdims=True)
        stats[2] = stats[2] * fade + jnp.sum(weights * dprobs, axis=0, keepdims=True)
        return carry

    lax.fori_loop(0, na, look, 0)

    stats_in = sem["stats_in"]
    swap = copy(stats, stats_in, "stat", 0, c_peer)
    swap.start()
    swap.wait_recv()
    high = jnp.maximum(stats[0], stats_in[0])
    here, there = jnp.exp2(stats[0] - high), jnp.exp2(stats_in[0] - high)
    denom = stats[1] * here + stats_in[1] * there
    log_total = high + jnp.log2(denom)
    row_dot = (stats[2] * here + stats_in[2] * there) / denom

    def k1_copy(step):
        return copy(k_out.at[step, 1 - y], yk_in.at[step], "k1", step, y_peer)

    def v1_copy(step, r):
        at = step * nx + r
        return copy(v_out.at[step, :, xor(x, r, x_bits)], xv_in.at[at], "v1", at, x_peer(r))

    def k2_copy(step, r):
        at = step * nx + r
        return copy(xk_out.at[at], xk_in.at[at], "k2", at, x_peer(r))

    def v2_copy(step):
        return copy(yv_out.at[step], yv_in.at[step], "v2", step, y_peer)

    def ra_copy(step):
        return copy(a_out.at[step], a_in.at[step], "ra", step, a_peer(step))

    def grads(step):
        probs = jnp.exp2(sbuf[step] - log_total)
        dscores = (probs * (dpbuf[step] - row_dot)).astype(BF16)
        dk = dot(dscores, qs[...], 1, 0) * inv_root
        dv = dot(probs.astype(BF16), gs[...], 1, 0)
        dk = dk.reshape(SIDES, nx, rows, 128)
        dv = dv.reshape(SIDES, nx, rows, 128)
        k_out[step] = dk.astype(BF16)
        v_out[step] = dv.astype(BF16)
        k1_copy(step).start()
        for r in range(1, nx):
            v1_copy(step, r).start()
        acck[step] = dk
        accv[step] = dv
        part = dot(chunk_of(step, 0), dscores, 0, 0)
        for k in range(CORES):
            dqt[k] += part[:, k * lanes : (k + 1) * lanes]

    def second(step):
        k1_copy(step).wait_recv()
        for r in range(1, nx):
            xx = xor(x, r, x_bits)
            both_y = acck[step, y, xx] + yk_in[step, xx].astype(F32)
            xk_out[step * nx + r] = both_y.astype(BF16)
            k2_copy(step, r).start()
        other, here_v = accv[step, 1 - y, x], accv[step, y, x]
        for r in range(1, nx):
            v1_copy(step, r).wait_recv()
            other = other + xv_in[step * nx + r, 1 - y].astype(F32)
            here_v = here_v + xv_in[step * nx + r, y].astype(F32)
        yv_out[step] = other.astype(BF16)
        v2_copy(step).start()
        a_own[step, 0] = acck[step, y, x] + yk_in[step, x].astype(F32)
        a_own[step, 1] = here_v

    def third(step):
        total = a_own[step, 0]
        for r in range(1, nx):
            k2_copy(step, r).wait_recv()
            total = total + xk_in[step * nx + r].astype(F32)
        v2_copy(step).wait_recv()
        total_v = a_own[step, 1] + yv_in[step].astype(F32)
        a_own[step, 0] = total
        a_own[step, 1] = total_v

        @pl.when(step > 0)
        def _():
            a_out[step, 0] = total.astype(BF16)
            a_out[step, 1] = total_v.astype(BF16)
            ra_copy(step).start()

    def turn(i, carry):
        grads(na - 1 - i)

        @pl.when(i >= LAG)
        def _():
            second(na - 1 - i + LAG)

        @pl.when(i >= 2 * LAG)
        def _():
            third(na - 1 - i + 2 * LAG)

        return carry

    lax.fori_loop(0, na, turn, 0)
    dq_own = sem["dq_own"]
    swap_dq = copy(dqt.at[1 - c], dq_in, "dq", 0, c_peer)
    swap_dq.start()

    for step in range(min(LAG, na) - 1, -1, -1):
        second(step)
        if step + LAG < na:
            third(step + LAG)
    swap_dq.wait_recv()
    dq = jnp.transpose(dqt[c] + dq_in[...]) * inv_root
    for h in range(heads):
        dq_own[:, h * 128 : (h + 1) * 128] = dq[h * rows : (h + 1) * rows, :]
    results = [
        pltpu.make_async_copy(src, dst, sem["out"].at[i])
        for i, (src, dst) in enumerate([(dq_own, dq_ref), (sem["dk_own"], dk_ref), (sem["dv_own"], dv_ref)])
    ]
    results[0].start()

    for step in range(min(LAG, na) - 1, -1, -1):
        third(step)

    for one in first + share + [id_share] + facts + facts_fwd + facts_a + [swap, swap_dq]:
        one.wait_send()

    def sent(step, carry):
        @pl.when(step > 0)
        def _():
            for one in block_copies(step):
                one.wait_send()
            ra_copy(step).wait_send()

        for one in forwards(step):
            one.wait_send()
        k1_copy(step).wait_send()
        v2_copy(step).wait_send()
        for r in range(1, nx):
            v1_copy(step, r).wait_send()
            k2_copy(step, r).wait_send()
        return carry

    lax.fori_loop(0, na, sent, 0)

    def collect(step, carry):
        ra_copy(step).wait_recv()
        return carry + a_in[step].astype(F32)

    done = lax.fori_loop(1, na, collect, a_own[0])
    sem["dk_own"][...] = done[0]
    sem["dv_own"][...] = done[1]
    results[1].start()
    results[2].start()
    for one in results:
        one.wait()


def hand_over(*refs):
    count = (len(refs) - 1) // 2
    moves = [pltpu.make_async_copy(refs[i], refs[count + i], refs[-1].at[i]) for i in range(count)]
    for one in moves:
        one.start()
    for one in moves:
        one.wait()


def on_device(queries, key_vecs, value_vecs, out_grad, positions, documents):
    nx = lax.axis_size("head")
    na = lax.axis_size("ctx") // (CORES * SIDES)
    rows, width = queries.shape
    heads = width // 128
    seq = rows * nx * na * CORES * SIDES
    docs = max(2, seq // 1024)
    lanes, group = heads * rows, SIDES * nx
    chunk = group * rows
    wide = CORES * lanes
    dma = pltpu.SemaphoreType.DMA
    vmem = pltpu.VMEM
    copies = {
        "ak": na, "av": na, "ainf": na, "idq": 1, "y0k": 1, "y0v": 1, "x0k": nx, "x0v": nx, "qg": 2,
        "x": na * nx, "y": na, "fk": na * nx, "fv": na * nx, "xinf": nx, "yinf": 1, "finf": nx, "stat": 1,
        "k1": na, "v1": na * nx, "k2": na * nx, "v2": na, "dq": 1, "ra": na,
    }
    names, tail = [], []
    for name, count in copies.items():
        names += ["s_" + name, "r_" + name]
        tail += [dma((count,)), dma((count,))]
    names += ["own", "out", "info_q", "stats_in", "dq_own", "dk_own", "dv_own"]
    tail += [dma((6,)), dma((3,)), vmem((CORES, 1, 128), jnp.int32), vmem((3, 1, wide), F32)]
    tail += [vmem((rows, width), F32), vmem((rows, 128), F32), vmem((rows, 128), F32)]
    scratch = [
        vmem((2, CORES, rows, width), BF16),
        vmem((wide, 128), BF16),
        vmem((wide, 128), BF16),
        vmem((na, 2, SIDES, nx, rows, 128), BF16),
        vmem((na, SIDES, nx, docs + 1, 1, 128), jnp.int32),
        vmem((2, 1, rows), jnp.int32),
        vmem((na, chunk, wide), F32),
        vmem((na, chunk, wide), F32),
        vmem((3, 1, wide), F32),
        vmem((CORES, 128, lanes), F32),
        vmem((128, lanes), F32),
        vmem((na, SIDES, nx, rows, 128), F32),
        vmem((na, SIDES, nx, rows, 128), F32),
        vmem((na, SIDES, nx, rows, 128), BF16),
        vmem((na, nx, rows, 128), BF16),
        vmem((na, SIDES, nx, rows, 128), BF16),
        vmem((na * nx, SIDES, rows, 128), BF16),
        vmem((na * nx, rows, 128), BF16),
        vmem((na * nx, rows, 128), BF16),
        vmem((na, rows, 128), BF16),
        vmem((na, rows, 128), BF16),
        vmem((na, 2, rows, 128), BF16),
        vmem((na, 2, rows, 128), BF16),
        vmem((na, 2, rows, 128), F32),
    ] + tail
    cfg = (nx, na, rows, heads, docs, names)
    far = pl.BlockSpec(memory_space=pltpu.HBM)
    pairs = lanes * seq
    shapes = (
        jax.ShapeDtypeStruct((rows, width), F32),
        jax.ShapeDtypeStruct((rows, 128), F32),
        jax.ShapeDtypeStruct((rows, 128), F32),
    )
    found = pl.pallas_call(
        functools.partial(kernel, cfg),
        out_shape=shapes,
        in_specs=[far] * 6,
        out_specs=(far, far, far),
        scratch_shapes=scratch,
        compiler_params=pltpu.CompilerParams(
            collective_id=0, has_side_effects=True, vmem_limit_bytes=64 * 1024 * 1024
        ),
        cost_estimate=pl.CostEstimate(
            flops=10 * pairs * 128, bytes_accessed=rows * width * 8, transcendentals=2 * pairs
        ),
    )(queries, key_vecs, value_vecs, out_grad, positions.reshape(1, rows), documents.reshape(1, rows))
    return pl.pallas_call(
        hand_over,
        out_shape=shapes,
        in_specs=[pl.BlockSpec(memory_space=pltpu.VMEM)] * 3,
        out_specs=(far, far, far),
        scratch_shapes=[dma((3,))],
        compiler_params=pltpu.CompilerParams(vmem_limit_bytes=64 * 1024 * 1024),
    )(*found)


def solution(mesh):
    tokens = P(("head", "ctx"), None)
    ids = P(("head", "ctx"))
    return jax.shard_map(
        on_device,
        mesh=mesh,
        in_specs=(tokens, tokens, tokens, tokens, ids, ids),
        out_specs=(tokens, tokens, tokens),
        check_vma=False,
    )
```

time: 45.3 us -> 36.7 us (0.81)
  Pallas kernels: 44.5 us -> 35.9 us
    pallas_call x1, Pallas kernels: 11.1 us -> 1.71 us  [on_device(): pl.pallas_call(hand_over, out_shape=shapes, in_specs=[pl.BlockSpec(memory...]
    pallas_call x1, Pallas kernels: 33.4 us -> 34.2 us  [on_device(): pl.pallas_call(functools.partial(kernel, cfg), out_shape=shapes, in_specs...]
where the time goes in v3:
time: 36.7 us; the launch traced here: 36.5 us
  Pallas kernels  35.9 us (98%)
  between operations  0.64 us (2%)
    pallas_call x1, Pallas kernels, on_device(): pl.pallas_call(functools.partial(kernel, cfg), out_shape=shapes, in_specs...  34.2 us
    pallas_call x1, Pallas kernels, on_device(): pl.pallas_call(hand_over, out_shape=shapes, in_specs=[pl.BlockSpec(memory...  1.71 us

profile of v3, /device:TPU:0, one launch (start us, length us, event | category | flops | bytes accessed | tf_op | source)
XLA Modules:
  0.0 36.5 jit_solution(8154600554743231154)
XLA Ops:
  0.6 34.2 %shard_map.85 = (f32[64,1024]{1,0:T(8,128)}, f32[64,128]{1,0:T(8,128)}, f32[64,128]{1,0:T(8,128)}) custom-call(bf16[64,1024]{1,0:T(8,128)(2,1)} %q_ref.1, bf16[64,128]{1,0:T(8,128)(2,1)} %k_ref.1, bf16[64,128]{1,0:T(8,128)(2,1)} %v_ref.1, bf16[64,1024]{1,0:T(8,128)(2,1)} %g_ref.1, s32[1,64]{1,0:T(1,128)} %bitcast.2, s32[1,64]{1,0:T(1,128)} %bitcast.3), custom_call_target="tpu_custom_call" | custom-call | flops 1342177280 | bytes 524288 | tf_op jit(solution)/shard_map/pallas_call | solution.py:456
  34.8 1.7 %shard_map.86 = (f32[64,1024]{1,0:T(8,128)}, f32[64,128]{1,0:T(8,128)}, f32[64,128]{1,0:T(8,128)}) custom-call(f32[64,1024]{1,0:T(8,128)} %get-tuple-element.6.refs_0_, f32[64,128]{1,0:T(8,128)} %get-tuple-element.7.refs_1_, f32[64,128]{1,0:T(8,128)} %get-tuple-element.8.refs_2_), custom_call_target="tpu_custom_call" | custom-call | tf_op jit(solution)/shard_map/pallas_call | solution.py:469

commit v4 on v3

v4 whole, which is shorter than its diff:
```python
import functools
import math

import jax
import jax.numpy as jnp
from jax import lax
from jax.experimental import pallas as pl
from jax.experimental.pallas import tpu as pltpu
from jax.sharding import PartitionSpec as P

MESH = pl.DeviceIdType.MESH
NEG_BIG = -1e30
CORES = 2
LAG = 2
SIDES = 2
F32 = jnp.float32
BF16 = jnp.bfloat16


def dot(lhs, rhs, lhs_dim, rhs_dim):
    return lax.dot_general(
        lhs, rhs, (((lhs_dim,), (rhs_dim,)), ((), ())), preferred_element_type=F32
    )


def xor(left, right, bits):
    total = 0
    for b in range(bits):
        total = total + ((left // 2**b + right // 2**b) % 2) * 2**b
    return total


def kernel(
    cfg,
    q_ref, k_ref, v_ref, g_ref, pos_ref, doc_ref,
    dq_ref, dk_ref, dv_ref,
    raw, qs, gs, qt, gt, kv, info, ids, sbuf, dpbuf, stats, dqt, dq_in, acc, g_out, g_in, a_out, a_in, a_own,
    *sems,
):
    nx, na, rows, heads, docs, names = cfg
    sem = dict(zip(names, sems))
    lanes = heads * rows
    group = SIDES * nx
    x_bits, a_bits = (nx - 1).bit_length(), (na - 1).bit_length()
    inv_root = 1.0 / math.sqrt(128)
    scale = inv_root * math.log2(math.e)

    x = lax.axis_index("head")
    ctx = lax.axis_index("ctx")
    a, y, c = ctx // 4, (ctx // 2) % 2, ctx % 2

    def a_peer(r):
        return (x, xor(a, r, a_bits) * 4 + y * 2 + c)

    def group_place(r):
        return ((y + r // nx) % SIDES, xor(x, r % nx, x_bits))

    def group_peer(r):
        yy, xx = group_place(r)
        return (xx, a * 4 + yy * 2 + c)

    c_peer = (x, a * 4 + y * 2 + 1 - c)

    def copy(src, dst, name, at, to):
        send, recv = sem["s_" + name], sem["r_" + name]
        return pltpu.make_async_remote_copy(
            src_ref=src, dst_ref=dst, send_sem=send.at[at], recv_sem=recv.at[at], device_id=to, device_id_type=MESH
        )

    barrier = pltpu.get_barrier_semaphore()
    everyone = [a_peer(r) for r in range(1, na)] + [group_peer(r) for r in range(1, group)] + [c_peer]
    for to in everyone:
        pl.semaphore_signal(barrier, inc=1, device_id=to, device_id_type=MESH)

    own_slot = kv.at[a, :, y, x]
    own = [
        pltpu.make_async_copy(src, dst, sem["own"].at[i])
        for i, (src, dst) in enumerate([
            (pos_ref, ids.at[0]), (doc_ref, ids.at[1]),
            (k_ref, kv.at[a, 0, y, x]), (v_ref, kv.at[a, 1, y, x]),
            (q_ref, raw.at[0, c]), (g_ref, raw.at[1, c]),
        ])
    ]
    for one in own:
        one.start()

    pl.semaphore_wait(barrier, len(everyone))

    def a_copy(step):
        return copy(own_slot, own_slot, "a", step, a_peer(step))

    def group_copies(step):
        block = kv.at[xor(a, step, a_bits), :, y, x]
        return [copy(block, block, "g", step * group + r, group_peer(r)) for r in range(1, group)]

    def send_all(copies):
        for one in copies:
            one.start()

    own[2].wait()
    own[3].wait()
    first = [a_copy(r) for r in range(1, na)]
    send_all(first)
    send_all(group_copies(0))

    share = [copy(q_ref, raw.at[0, c], "qg", 0, c_peer), copy(g_ref, raw.at[1, c], "qg", 1, c_peer)]
    for one in share:
        one.start()

    fields = docs + 1
    own[0].wait()
    own[1].wait()
    pos_own = ids[0]
    doc_own = ids[1]
    info[a, y, x, 0] = jnp.broadcast_to(pos_own[:, 0:1], (1, 128))
    for d in range(docs):
        tally = jnp.sum(jnp.where(doc_own == d, 1, 0), axis=1, keepdims=True)
        info[a, y, x, 1 + d] = jnp.broadcast_to(tally, (1, 128))
    info_slot = info.at[a, y, x]
    facts = [copy(info_slot, info_slot, "ginf", r, group_peer(r)) for r in range(1, group)]
    spare = 128 - 2 * rows
    pieces = [pos_own, doc_own] + ([jnp.zeros((1, spare), jnp.int32)] if spare else [])
    info_q = sem["info_q"]
    info_q[c] = jnp.concatenate(pieces, axis=1)
    id_share = copy(info_q.at[c], info_q.at[c], "idq", 0, c_peer)
    for one in facts + [id_share]:
        one.start()

    def relay(step):
        a_copy(step).wait_recv()
        send_all(group_copies(step))

    facts_a = [copy(info.at[a], info.at[a], "ainf", r, a_peer(r)) for r in range(1, na)]
    for one in facts:
        one.wait_recv()
    send_all(facts_a)
    for one in own[4:]:
        one.wait()
    for one in share + [id_share]:
        one.wait_recv()
    for k in range(CORES):
        for h in range(heads):
            at = k * lanes + h * rows
            qs[at : at + rows, :] = raw[0, k, :, h * 128 : (h + 1) * 128]
            gs[at : at + rows, :] = raw[1, k, :, h * 128 : (h + 1) * 128]
    for step in range(1, min(3, na)):
        relay(step)
    qt[...] = jnp.transpose(qs[...])
    gt[...] = jnp.transpose(gs[...])
    both = [info_q[k] for k in range(CORES)]
    pos_q = jnp.concatenate([one[:, :rows] for one in both for _ in range(heads)], axis=1)
    doc_q = jnp.concatenate([one[:, rows : 2 * rows] for one in both for _ in range(heads)], axis=1)
    wide = CORES * lanes
    stats[0] = jnp.full((1, wide), NEG_BIG, F32)
    stats[1] = jnp.zeros((1, wide), F32)
    stats[2] = jnp.zeros((1, wide), F32)
    dqt[...] = jnp.zeros(dqt.shape, F32)

    row_ids = lax.broadcasted_iota(jnp.int32, (rows, wide), 0)

    def widen(row):
        return jnp.concatenate([row] * (wide // 128), axis=1)

    def chunk_of(step, which):
        return kv[xor(a, step, a_bits), which].reshape(group * rows, 128)

    def look(step, carry):
        @pl.when((step >= 1) & (step + 2 < na))
        def _():
            relay(step + 2)

        @pl.when(step == 1)
        def _():
            for one in facts_a:
                one.wait_recv()

        for one in group_copies(step):
            one.wait_recv()

        scores = dot(chunk_of(step, 0), qt[...], 1, 0)
        dprobs = dot(chunk_of(step, 1), gt[...], 1, 0)
        old = stats[0]
        high = old
        at = xor(a, step, a_bits)
        for b in range(group):
            row = lambda f: widen(info[at, b // nx, b % nx, f])
            upper = pos_q - row(0)
            lower = jnp.zeros((1, wide), jnp.int32)
            for d in range(docs):
                lower = lower + jnp.where(doc_q > d, row(1 + d), 0)
            seen = (row_ids >= lower) & (row_ids <= upper)
            part = jnp.where(seen, scores[b * rows : (b + 1) * rows, :] * scale, NEG_BIG)
            sbuf[step, b * rows : (b + 1) * rows, :] = part
            high = jnp.maximum(high, jnp.max(part, axis=0, keepdims=True))
        dpbuf[step] = dprobs
        fade = jnp.exp2(old - high)
        weights = jnp.exp2(sbuf[step] - high)
        stats[0] = high
        stats[1] = stats[1] * fade + jnp.sum(weights, axis=0, keepdims=True)
        stats[2] = stats[2] * fade + jnp.sum(weights * dprobs, axis=0, keepdims=True)
        return carry

    lax.fori_loop(0, na, look, 0)

    stats_in = sem["stats_in"]
    swap = copy(stats, stats_in, "stat", 0, c_peer)
    swap.start()
    swap.wait_recv()
    high = jnp.maximum(stats[0], stats_in[0])
    here, there = jnp.exp2(stats[0] - high), jnp.exp2(stats_in[0] - high)
    denom = stats[1] * here + stats_in[1] * there
    log_total = high + jnp.log2(denom)
    row_dot = (stats[2] * here + stats_in[2] * there) / denom

    def sum_copies(step):
        found = []
        for r in range(1, group):
            yy, xx = group_place(r)
            at = step * group + r
            found.append(copy(g_out.at[step, :, yy, xx], g_in.at[at], "sum", at, group_peer(r)))
        return found

    def ra_copy(step):
        return copy(a_out.at[step], a_in.at[step], "ra", step, a_peer(step))

    def grads(step):
        probs = jnp.exp2(sbuf[step] - log_total)
        dscores = (probs * (dpbuf[step] - row_dot)).astype(BF16)
        dk = dot(dscores, qs[...], 1, 0) * inv_root
        dv = dot(probs.astype(BF16), gs[...], 1, 0)
        for which, one in enumerate((dk, dv)):
            one = one.reshape(SIDES, nx, rows, 128)
            g_out[step, which] = one.astype(BF16)
            acc[step, which] = one
        send_all(sum_copies(step))
        part = dot(chunk_of(step, 0), dscores, 0, 0)
        for k in range(CORES):
            dqt[k] += part[:, k * lanes : (k + 1) * lanes]

    def second(step):
        total = acc[step, :, y, x]
        for r, one in enumerate(sum_copies(step)):
            one.wait_recv()
            total = total + g_in[step * group + r + 1].astype(F32)
        a_own[step] = total

        @pl.when(step > 0)
        def _():
            a_out[step] = total.astype(BF16)
            ra_copy(step).start()

    def turn(i, carry):
        grads(na - 1 - i)

        @pl.when(i >= LAG)
        def _():
            second(na - 1 - i + LAG)

        return carry

    lax.fori_loop(0, na, turn, 0)
    dq_own = sem["dq_own"]
    swap_dq = copy(dqt.at[1 - c], dq_in, "dq", 0, c_peer)
    swap_dq.start()

    for step in range(min(LAG, na) - 1, 0, -1):
        second(step)
    swap_dq.wait_recv()
    dq = jnp.transpose(dqt[c] + dq_in[...]) * inv_root
    for h in range(heads):
        dq_own[:, h * 128 : (h + 1) * 128] = dq[h * rows : (h + 1) * rows, :]
    results = [
        pltpu.make_async_copy(src, dst, sem["out"].at[i])
        for i, (src, dst) in enumerate([(dq_own, dq_ref), (sem["dk_own"], dk_ref), (sem["dv_own"], dv_ref)])
    ]
    results[0].start()

    second(0)

    for one in first + share + [id_share] + facts + facts_a + [swap, swap_dq]:
        one.wait_send()

    def sent(step, carry):
        @pl.when(step > 0)
        def _():
            ra_copy(step).wait_send()

        for one in group_copies(step) + sum_copies(step):
            one.wait_send()
        return carry

    lax.fori_loop(0, na, sent, 0)

    def collect(step, carry):
        ra_copy(step).wait_recv()
        return carry + a_in[step].astype(F32)

    done = lax.fori_loop(1, na, collect, a_own[0])
    sem["dk_own"][...] = done[0]
    sem["dv_own"][...] = done[1]
    results[1].start()
    results[2].start()
    for one in results:
        one.wait()


def hand_over(*refs):
    count = (len(refs) - 1) // 2
    moves = [pltpu.make_async_copy(refs[i], refs[count + i], refs[-1].at[i]) for i in range(count)]
    for one in moves:
        one.start()
    for one in moves:
        one.wait()


def on_device(queries, key_vecs, value_vecs, out_grad, positions, documents):
    nx = lax.axis_size("head")
    na = lax.axis_size("ctx") // (CORES * SIDES)
    rows, width = queries.shape
    heads = width // 128
    seq = rows * nx * na * CORES * SIDES
    docs = max(2, seq // 1024)
    lanes, group = heads * rows, SIDES * nx
    chunk = group * rows
    wide = CORES * lanes
    dma = pltpu.SemaphoreType.DMA
    vmem = pltpu.VMEM
    copies = {
        "a": na, "g": na * group, "ginf": group, "ainf": na, "idq": 1, "qg": 2, "stat": 1,
        "sum": na * group, "ra": na, "dq": 1,
    }
    names, tail = [], []
    for name, count in copies.items():
        names += ["s_" + name, "r_" + name]
        tail += [dma((count,)), dma((count,))]
    names += ["own", "out", "info_q", "stats_in", "dq_own", "dk_own", "dv_own"]
    tail += [dma((6,)), dma((3,)), vmem((CORES, 1, 128), jnp.int32), vmem((3, 1, wide), F32)]
    tail += [vmem((rows, width), F32), vmem((rows, 128), F32), vmem((rows, 128), F32)]
    scratch = [
        vmem((2, CORES, rows, width), BF16),
        vmem((wide, 128), BF16),
        vmem((wide, 128), BF16),
        vmem((128, wide), BF16),
        vmem((128, wide), BF16),
        vmem((na, 2, SIDES, nx, rows, 128), BF16),
        vmem((na, SIDES, nx, docs + 1, 1, 128), jnp.int32),
        vmem((2, 1, rows), jnp.int32),
        vmem((na, chunk, wide), F32),
        vmem((na, chunk, wide), F32),
        vmem((3, 1, wide), F32),
        vmem((CORES, 128, lanes), F32),
        vmem((128, lanes), F32),
        vmem((na, 2, SIDES, nx, rows, 128), F32),
        vmem((na, 2, SIDES, nx, rows, 128), BF16),
        vmem((na * group, 2, rows, 128), BF16),
        vmem((na, 2, rows, 128), BF16),
        vmem((na, 2, rows, 128), BF16),
        vmem((na, 2, rows, 128), F32),
    ] + tail
    cfg = (nx, na, rows, heads, docs, names)
    far = pl.BlockSpec(memory_space=pltpu.HBM)
    pairs = lanes * seq
    shapes = (
        jax.ShapeDtypeStruct((rows, width), F32),
        jax.ShapeDtypeStruct((rows, 128), F32),
        jax.ShapeDtypeStruct((rows, 128), F32),
    )
    found = pl.pallas_call(
        functools.partial(kernel, cfg),
        out_shape=shapes,
        in_specs=[far] * 6,
        out_specs=(far, far, far),
        scratch_shapes=scratch,
        compiler_params=pltpu.CompilerParams(
            collective_id=0, has_side_effects=True, vmem_limit_bytes=64 * 1024 * 1024
        ),
        cost_estimate=pl.CostEstimate(
            flops=10 * pairs * 128, bytes_accessed=rows * width * 8, transcendentals=2 * pairs
        ),
    )(queries, key_vecs, value_vecs, out_grad, positions.reshape(1, rows), documents.reshape(1, rows))
    return pl.pallas_call(
        hand_over,
        out_shape=shapes,
        in_specs=[pl.BlockSpec(memory_space=pltpu.VMEM)] * 3,
        out_specs=(far, far, far),
        scratch_shapes=[dma((3,))],
        compiler_params=pltpu.CompilerParams(vmem_limit_bytes=64 * 1024 * 1024),
    )(*found)


def solution(mesh):
    tokens = P(("head", "ctx"), None)
    ids = P(("head", "ctx"))
    return jax.shard_map(
        on_device,
        mesh=mesh,
        in_specs=(tokens, tokens, tokens, tokens, ids, ids),
        out_specs=(tokens, tokens, tokens),
        check_vma=False,
    )
```

time: 36.7 us -> 29.8 us (0.81)
  Pallas kernels: 35.9 us -> 29 us
    pallas_call x1, Pallas kernels: 34.2 us -> 27.3 us  [on_device(): pl.pallas_call(functools.partial(kernel, cfg), out_shape=shapes, in_specs...]
where the time goes in v4:
time: 29.8 us; the launch traced here: 29.6 us
  Pallas kernels  29 us (97%)
  between operations  0.64 us (2%)
    pallas_call x1, Pallas kernels, on_device(): pl.pallas_call(functools.partial(kernel, cfg), out_shape=shapes, in_specs...  27.3 us
    pallas_call x1, Pallas kernels, on_device(): pl.pallas_call(hand_over, out_shape=shapes, in_specs=[pl.BlockSpec(memory...  1.71 us

profile of v4, /device:TPU:0, one launch (start us, length us, event | category | flops | bytes accessed | tf_op | source)
XLA Modules:
  0.0 29.6 jit_solution(10025303162409852233)
XLA Ops:
  0.6 27.3 %shard_map.85 = (f32[64,1024]{1,0:T(8,128)}, f32[64,128]{1,0:T(8,128)}, f32[64,128]{1,0:T(8,128)}) custom-call(bf16[64,1024]{1,0:T(8,128)(2,1)} %q_ref.1, bf16[64,128]{1,0:T(8,128)(2,1)} %k_ref.1, bf16[64,128]{1,0:T(8,128)(2,1)} %v_ref.1, bf16[64,1024]{1,0:T(8,128)(2,1)} %g_ref.1, s32[1,64]{1,0:T(1,128)} %bitcast.2, s32[1,64]{1,0:T(1,128)} %bitcast.3), custom_call_target="tpu_custom_call" | custom-call | flops 1342177280 | bytes 524288 | tf_op jit(solution)/shard_map/pallas_call | solution.py:368
  27.9 1.7 %shard_map.86 = (f32[64,1024]{1,0:T(8,128)}, f32[64,128]{1,0:T(8,128)}, f32[64,128]{1,0:T(8,128)}) custom-call(f32[64,1024]{1,0:T(8,128)} %get-tuple-element.6.refs_0_, f32[64,128]{1,0:T(8,128)} %get-tuple-element.7.refs_1_, f32[64,128]{1,0:T(8,128)} %get-tuple-element.8.refs_2_), custom_call_target="tpu_custom_call" | custom-call | tf_op jit(solution)/shard_map/pallas_call | solution.py:381

commit v5 on v4

--- a/solution.py
+++ b/solution.py
@@ -11,6 +11,7 @@
 MESH = pl.DeviceIdType.MESH
 NEG_BIG = -1e30
 CORES = 2
+TILE = 256
 LAG = 2
 SIDES = 2
 F32 = jnp.float32
@@ -156,10 +157,12 @@
     stats[2] = jnp.zeros((1, wide), F32)
     dqt[...] = jnp.zeros(dqt.shape, F32)
 
-    row_ids = lax.broadcasted_iota(jnp.int32, (rows, wide), 0)
+    tile = min(TILE, wide)
+    tiles = [slice(t, t + tile) for t in range(0, wide, tile)]
+    row_ids = lax.broadcasted_iota(jnp.int32, (rows, tile), 0)
 
     def widen(row):
-        return jnp.concatenate([row] * (wide // 128), axis=1)
+        return jnp.concatenate([row] * (tile // 128), axis=1)
 
     def chunk_of(step, which):
         return kv[xor(a, step, a_bits), which].reshape(group * rows, 128)
@@ -177,27 +180,29 @@
         for one in group_copies(step):
             one.wait_recv()
 
-        scores = dot(chunk_of(step, 0), qt[...], 1, 0)
-        dprobs = dot(chunk_of(step, 1), gt[...], 1, 0)
-        old = stats[0]
-        high = old
+        keys, values = chunk_of(step, 0), chunk_of(step, 1)
         at = xor(a, step, a_bits)
-        for b in range(group):
-            row = lambda f: widen(info[at, b // nx, b % nx, f])
-            upper = pos_q - row(0)
-            lower = jnp.zeros((1, wide), jnp.int32)
-            for d in range(docs):
-                lower = lower + jnp.where(doc_q > d, row(1 + d), 0)
-            seen = (row_ids >= lower) & (row_ids <= upper)
-            part = jnp.where(seen, scores[b * rows : (b + 1) * rows, :] * scale, NEG_BIG)
-            sbuf[step, b * rows : (b + 1) * rows, :] = part
-            high = jnp.maximum(high, jnp.max(part, axis=0, keepdims=True))
-        dpbuf[step] = dprobs
-        fade = jnp.exp2(old - high)
-        weights = jnp.exp2(sbuf[step] - high)
-        stats[0] = high
-        stats[1] = stats[1] * fade + jnp.sum(weights, axis=0, keepdims=True)
-        stats[2] = stats[2] * fade + jnp.sum(weights * dprobs, axis=0, keepdims=True)
+        for cols in tiles:
+            scores = dot(keys, qt[:, cols], 1, 0)
+            old = stats[0, :, cols]
+            high = old
+            for b in range(group):
+                row = lambda f: widen(info[at, b // nx, b % nx, f])
+                upper = pos_q[:, cols] - row(0)
+                lower = jnp.zeros((1, tile), jnp.int32)
+                for d in range(docs):
+                    lower = lower + jnp.where(doc_q[:, cols] > d, row(1 + d), 0)
+                seen = (row_ids >= lower) & (row_ids <= upper)
+                part = jnp.where(seen, scores[b * rows : (b + 1) * rows, :] * scale, NEG_BIG)
+                sbuf[step, b * rows : (b + 1) * rows, cols] = part
+                high = jnp.maximum(high, jnp.max(part, axis=0, keepdims=True))
+            dprobs = dot(values, gt[:, cols], 1, 0)
+            dpbuf[step, :, cols] = dprobs
+            fade = jnp.exp2(old - high)
+            weights = jnp.exp2(sbuf[step, :, cols] - high)
+            stats[0, :, cols] = high
+            stats[1, :, cols] = stats[1, :, cols] * fade + jnp.sum(weights, axis=0, keepdims=True)
+            stats[2, :, cols] = stats[2, :, cols] * fade + jnp.sum(weights * dprobs, axis=0, keepdims=True)
         return carry
 
     lax.fori_loop(0, na, look, 0)
@@ -224,18 +229,21 @@
         return copy(a_out.at[step], a_in.at[step], "ra", step, a_peer(step))
 
     def grads(step):
-        probs = jnp.exp2(sbuf[step] - log_total)
-        dscores = (probs * (dpbuf[step] - row_dot)).astype(BF16)
-        dk = dot(dscores, qs[...], 1, 0) * inv_root
-        dv = dot(probs.astype(BF16), gs[...], 1, 0)
+        keys = chunk_of(step, 0)
+        for cols in tiles:
+            probs = jnp.exp2(sbuf[step, :, cols] - log_total[:, cols])
+            dscores = (probs * (dpbuf[step, :, cols] - row_dot[:, cols])).astype(BF16)
+            sem["probs"][:, cols] = probs.astype(BF16)
+            sem["dscores"][:, cols] = dscores
+        dk = dot(sem["dscores"][...], qs[...], 1, 0) * inv_root
+        dv = dot(sem["probs"][...], gs[...], 1, 0)
         for which, one in enumerate((dk, dv)):
             one = one.reshape(SIDES, nx, rows, 128)
             g_out[step, which] = one.astype(BF16)
             acc[step, which] = one
         send_all(sum_copies(step))
-        part = dot(chunk_of(step, 0), dscores, 0, 0)
         for k in range(CORES):
-            dqt[k] += part[:, k * lanes : (k + 1) * lanes]
+            dqt[k] += dot(keys, sem["dscores"][:, k * lanes : (k + 1) * lanes], 0, 0)
 
     def second(step):
         total = acc[step, :, y, x]
@@ -259,7 +267,6 @@
         return carry
 
     lax.fori_loop(0, na, turn, 0)
-    dq_own = sem["dq_own"]
     swap_dq = copy(dqt.at[1 - c], dq_in, "dq", 0, c_peer)
     swap_dq.start()
 
@@ -268,13 +275,7 @@
     swap_dq.wait_recv()
     dq = jnp.transpose(dqt[c] + dq_in[...]) * inv_root
     for h in range(heads):
-        dq_own[:, h * 128 : (h + 1) * 128] = dq[h * rows : (h + 1) * rows, :]
-    results = [
-        pltpu.make_async_copy(src, dst, sem["out"].at[i])
-        for i, (src, dst) in enumerate([(dq_own, dq_ref), (sem["dk_own"], dk_ref), (sem["dv_own"], dv_ref)])
-    ]
-    results[0].start()
-
+        dq_ref[:, h * 128 : (h + 1) * 128] = dq[h * rows : (h + 1) * rows, :]
     second(0)
 
     for one in first + share + [id_share] + facts + facts_a + [swap, swap_dq]:
@@ -296,12 +297,8 @@
         return carry + a_in[step].astype(F32)
 
     done = lax.fori_loop(1, na, collect, a_own[0])
-    sem["dk_own"][...] = done[0]
-    sem["dv_own"][...] = done[1]
-    results[1].start()
-    results[2].start()
-    for one in results:
-        one.wait()
+    dk_ref[...] = done[0]
+    dv_ref[...] = done[1]
 
 
 def hand_over(*refs):
@@ -333,9 +330,9 @@
     for name, count in copies.items():
         names += ["s_" + name, "r_" + name]
         tail += [dma((count,)), dma((count,))]
-    names += ["own", "out", "info_q", "stats_in", "dq_own", "dk_own", "dv_own"]
-    tail += [dma((6,)), dma((3,)), vmem((CORES, 1, 128), jnp.int32), vmem((3, 1, wide), F32)]
-    tail += [vmem((rows, width), F32), vmem((rows, 128), F32), vmem((rows, 128), F32)]
+    names += ["own", "info_q", "stats_in", "probs", "dscores"]
+    tail += [dma((6,)), vmem((CORES, 1, 128), jnp.int32), vmem((3, 1, wide), F32)]
+    tail += [vmem((chunk, wide), BF16), vmem((chunk, wide), BF16)]
     scratch = [
         vmem((2, CORES, rows, width), BF16),
         vmem((wide, 128), BF16),
@@ -365,14 +362,15 @@
         jax.ShapeDtypeStruct((rows, 128), F32),
         jax.ShapeDtypeStruct((rows, 128), F32),
     )
+    near = pl.BlockSpec(memory_space=pltpu.VMEM)
     found = pl.pallas_call(
         functools.partial(kernel, cfg),
-        out_shape=shapes,
+        out_shape=tuple(pltpu.VMEM(one.shape, one.dtype) for one in shapes),
         in_specs=[far] * 6,
-        out_specs=(far, far, far),
+        out_specs=(near, near, near),
         scratch_shapes=scratch,
         compiler_params=pltpu.CompilerParams(
-            collective_id=0, has_side_effects=True, vmem_limit_bytes=64 * 1024 * 1024
+            collective_id=0, has_side_effects=True, vmem_limit_bytes=63 * 1024 * 1024
         ),
         cost_estimate=pl.CostEstimate(
             flops=10 * pairs * 128, bytes_accessed=rows * width * 8, transcendentals=2 * pairs
@@ -384,7 +382,7 @@
         in_specs=[pl.BlockSpec(memory_space=pltpu.VMEM)] * 3,
         out_specs=(far, far, far),
         scratch_shapes=[dma((3,))],
-        compiler_params=pltpu.CompilerParams(vmem_limit_bytes=64 * 1024 * 1024),
+        compiler_params=pltpu.CompilerParams(vmem_limit_bytes=1024 * 1024),
     )(*found)
 
 

time: 29.8 us -> 28.2 us (0.946)
  Pallas kernels: 29 us -> 27.4 us
    pallas_call x1, Pallas kernels: 1.71 us -> 0.74 us  [on_device(): pl.pallas_call(hand_over, out_shape=shapes, in_specs=[pl.BlockSpec(memory...]
    pallas_call x1, Pallas kernels: 27.3 us -> 26.7 us  [on_device(): pl.pallas_call(functools.partial(kernel, cfg), out_shape=tuple((pltpu.VME...]
where the time goes in v5:
time: 28.2 us; the launch traced here: 28.1 us
  Pallas kernels  27.4 us (97%)
  between operations  0.64 us (2%)
    pallas_call x1, Pallas kernels, on_device(): pl.pallas_call(functools.partial(kernel, cfg), out_shape=tuple((pltpu.VME...  26.7 us
    pallas_call x1, Pallas kernels, on_device(): pl.pallas_call(hand_over, out_shape=shapes, in_specs=[pl.BlockSpec(memory...  0.74 us

profile of v5, /device:TPU:0, one launch (start us, length us, event | category | flops | bytes accessed | tf_op | source)
XLA Modules:
  0.0 28.1 jit_solution(6828450855245993902)
XLA Ops:
  0.6 26.7 %shard_map.85 = (f32[64,1024]{1,0:T(8,128)S(1)}, f32[64,128]{1,0:T(8,128)S(1)}, f32[64,128]{1,0:T(8,128)S(1)}) custom-call(bf16[64,1024]{1,0:T(8,128)(2,1)} %q_ref.1, bf16[64,128]{1,0:T(8,128)(2,1)} %k_ref.1, bf16[64,128]{1,0:T(8,128)(2,1)} %v_ref.1, bf16[64,1024]{1,0:T(8,128)(2,1)} %g_ref.1, s32[1,64]{1,0:T(1,128)} %bitcast.2, s32[1,64]{1,0:T(1,128)} %bitcast.3), custom_call_target="tpu_custom_call" | custom-call | flops 1342177280 | bytes 524288 | tf_op jit(solution)/shard_map/pallas_call | solution.py:366
  27.3 0.7 %shard_map.86 = (f32[64,1024]{1,0:T(8,128)}, f32[64,128]{1,0:T(8,128)}, f32[64,128]{1,0:T(8,128)}) custom-call(f32[64,1024]{1,0:T(8,128)S(1)} %get-tuple-element.6.refs_0_, f32[64,128]{1,0:T(8,128)S(1)} %get-tuple-element.7.refs_1_, f32[64,128]{1,0:T(8,128)S(1)} %get-tuple-element.8.refs_2_), custom_call_target="tpu_custom_call" | custom-call | tf_op jit(solution)/shard_map/pallas_call | solution.py:379

commit v6 on v5

--- a/solution.py
+++ b/solution.py
@@ -12,6 +12,7 @@
 NEG_BIG = -1e30
 CORES = 2
 TILE = 256
+FACTS = 16
 LAG = 2
 SIDES = 2
 F32 = jnp.float32
@@ -35,7 +36,7 @@
     cfg,
     q_ref, k_ref, v_ref, g_ref, pos_ref, doc_ref,
     dq_ref, dk_ref, dv_ref,
-    raw, qs, gs, qt, gt, kv, info, ids, sbuf, dpbuf, stats, dqt, dq_in, acc, g_out, g_in, a_out, a_in, a_own,
+    raw, qs, gs, qt, gt, kv, ids, sbuf, dpbuf, stats, dqt, dq_in, acc, g_out, g_in, a_out, a_in, a_own,
     *sems,
 ):
     nx, na, rows, heads, docs, names = cfg
@@ -73,25 +74,39 @@
     for to in everyone:
         pl.semaphore_signal(barrier, inc=1, device_id=to, device_id_type=MESH)
 
-    own_slot = kv.at[a, :, y, x]
+    own_slot = kv.at[a, y, x]
     own = [
         pltpu.make_async_copy(src, dst, sem["own"].at[i])
         for i, (src, dst) in enumerate([
             (pos_ref, ids.at[0]), (doc_ref, ids.at[1]),
-            (k_ref, kv.at[a, 0, y, x]), (v_ref, kv.at[a, 1, y, x]),
+            (k_ref, kv.at[a, y, x, pl.ds(0, rows)]), (v_ref, kv.at[a, y, x, pl.ds(rows, rows)]),
             (q_ref, raw.at[0, c]), (g_ref, raw.at[1, c]),
         ])
     ]
     for one in own:
         one.start()
 
+    own[0].wait()
+    own[1].wait()
+    pos_own = ids[0].astype(F32)
+    doc_own = ids[1].astype(F32)
+    coarse = jnp.floor(pos_own[:, 0:1] * (1.0 / 128.0))
+    fields = [coarse, pos_own[:, 0:1] - coarse * 128.0]
+    for d in range(docs):
+        fields.append(jnp.sum(jnp.where(doc_own == d, 1.0, 0.0), axis=1, keepdims=True))
+    field_ids = lax.broadcasted_iota(jnp.int32, (FACTS, 128), 0)
+    table = jnp.zeros((FACTS, 128), F32)
+    for f, one in enumerate(fields):
+        table = jnp.where(field_ids == f, one, table)
+    kv[a, y, x, 2 * rows :, :] = table.astype(BF16)
+
     pl.semaphore_wait(barrier, len(everyone))
 
     def a_copy(step):
         return copy(own_slot, own_slot, "a", step, a_peer(step))
 
     def group_copies(step):
-        block = kv.at[xor(a, step, a_bits), :, y, x]
+        block = kv.at[xor(a, step, a_bits), y, x]
         return [copy(block, block, "g", step * group + r, group_peer(r)) for r in range(1, group)]
 
     def send_all(copies):
@@ -108,33 +123,17 @@
     for one in share:
         one.start()
 
-    fields = docs + 1
-    own[0].wait()
-    own[1].wait()
-    pos_own = ids[0]
-    doc_own = ids[1]
-    info[a, y, x, 0] = jnp.broadcast_to(pos_own[:, 0:1], (1, 128))
-    for d in range(docs):
-        tally = jnp.sum(jnp.where(doc_own == d, 1, 0), axis=1, keepdims=True)
-        info[a, y, x, 1 + d] = jnp.broadcast_to(tally, (1, 128))
-    info_slot = info.at[a, y, x]
-    facts = [copy(info_slot, info_slot, "ginf", r, group_peer(r)) for r in range(1, group)]
     spare = 128 - 2 * rows
-    pieces = [pos_own, doc_own] + ([jnp.zeros((1, spare), jnp.int32)] if spare else [])
+    pieces = [pos_own, doc_own] + ([jnp.zeros((1, spare), F32)] if spare else [])
     info_q = sem["info_q"]
     info_q[c] = jnp.concatenate(pieces, axis=1)
     id_share = copy(info_q.at[c], info_q.at[c], "idq", 0, c_peer)
-    for one in facts + [id_share]:
-        one.start()
+    id_share.start()
 
     def relay(step):
         a_copy(step).wait_recv()
         send_all(group_copies(step))
 
-    facts_a = [copy(info.at[a], info.at[a], "ainf", r, a_peer(r)) for r in range(1, na)]
-    for one in facts:
-        one.wait_recv()
-    send_all(facts_a)
     for one in own[4:]:
         one.wait()
     for one in share + [id_share]:
@@ -159,39 +158,36 @@
 
     tile = min(TILE, wide)
     tiles = [slice(t, t + tile) for t in range(0, wide, tile)]
-    row_ids = lax.broadcasted_iota(jnp.int32, (rows, tile), 0)
+    row_ids = lax.broadcasted_iota(jnp.int32, (rows, tile), 0).astype(F32)
 
     def widen(row):
         return jnp.concatenate([row] * (tile // 128), axis=1)
 
     def chunk_of(step, which):
-        return kv[xor(a, step, a_bits), which].reshape(group * rows, 128)
+        part = slice(which * rows, (which + 1) * rows)
+        return kv[xor(a, step, a_bits), :, :, part, :].reshape(group * rows, 128)
 
     def look(step, carry):
         @pl.when((step >= 1) & (step + 2 < na))
         def _():
             relay(step + 2)
 
-        @pl.when(step == 1)
-        def _():
-            for one in facts_a:
-                one.wait_recv()
-
         for one in group_copies(step):
             one.wait_recv()
 
         keys, values = chunk_of(step, 0), chunk_of(step, 1)
         at = xor(a, step, a_bits)
+        tables = [kv[at, b // nx, b % nx, 2 * rows :, :].astype(F32) for b in range(group)]
         for cols in tiles:
             scores = dot(keys, qt[:, cols], 1, 0)
             old = stats[0, :, cols]
             high = old
             for b in range(group):
-                row = lambda f: widen(info[at, b // nx, b % nx, f])
-                upper = pos_q[:, cols] - row(0)
-                lower = jnp.zeros((1, tile), jnp.int32)
+                row = lambda f: widen(tables[b][f : f + 1, :])
+                upper = pos_q[:, cols] - row(0) * 128.0 - row(1)
+                lower = jnp.zeros((1, tile), F32)
                 for d in range(docs):
-                    lower = lower + jnp.where(doc_q[:, cols] > d, row(1 + d), 0)
+                    lower = lower + jnp.where(doc_q[:, cols] > d, row(2 + d), 0.0)
                 seen = (row_ids >= lower) & (row_ids <= upper)
                 part = jnp.where(seen, scores[b * rows : (b + 1) * rows, :] * scale, NEG_BIG)
                 sbuf[step, b * rows : (b + 1) * rows, cols] = part
@@ -229,7 +225,7 @@
         return copy(a_out.at[step], a_in.at[step], "ra", step, a_peer(step))
 
     def grads(step):
-        keys = chunk_of(step, 0)
+        keys_t = jnp.transpose(chunk_of(step, 0))
         for cols in tiles:
             probs = jnp.exp2(sbuf[step, :, cols] - log_total[:, cols])
             dscores = (probs * (dpbuf[step, :, cols] - row_dot[:, cols])).astype(BF16)
@@ -243,7 +239,7 @@
             acc[step, which] = one
         send_all(sum_copies(step))
         for k in range(CORES):
-            dqt[k] += dot(keys, sem["dscores"][:, k * lanes : (k + 1) * lanes], 0, 0)
+            dqt[k] += dot(keys_t, sem["dscores"][:, k * lanes : (k + 1) * lanes], 1, 0)
 
     def second(step):
         total = acc[step, :, y, x]
@@ -278,7 +274,7 @@
         dq_ref[:, h * 128 : (h + 1) * 128] = dq[h * rows : (h + 1) * rows, :]
     second(0)
 
-    for one in first + share + [id_share] + facts + facts_a + [swap, swap_dq]:
+    for one in first + share + [id_share] + [swap, swap_dq]:
         one.wait_send()
 
     def sent(step, carry):
@@ -323,7 +319,7 @@
     dma = pltpu.SemaphoreType.DMA
     vmem = pltpu.VMEM
     copies = {
-        "a": na, "g": na * group, "ginf": group, "ainf": na, "idq": 1, "qg": 2, "stat": 1,
+        "a": na, "g": na * group, "idq": 1, "qg": 2, "stat": 1,
         "sum": na * group, "ra": na, "dq": 1,
     }
     names, tail = [], []
@@ -331,7 +327,7 @@
         names += ["s_" + name, "r_" + name]
         tail += [dma((count,)), dma((count,))]
     names += ["own", "info_q", "stats_in", "probs", "dscores"]
-    tail += [dma((6,)), vmem((CORES, 1, 128), jnp.int32), vmem((3, 1, wide), F32)]
+    tail += [dma((6,)), vmem((CORES, 1, 128), F32), vmem((3, 1, wide), F32)]
     tail += [vmem((chunk, wide), BF16), vmem((chunk, wide), BF16)]
     scratch = [
         vmem((2, CORES, rows, width), BF16),
@@ -339,8 +335,7 @@
         vmem((wide, 128), BF16),
         vmem((128, wide), BF16),
         vmem((128, wide), BF16),
-        vmem((na, 2, SIDES, nx, rows, 128), BF16),
-        vmem((na, SIDES, nx, docs + 1, 1, 128), jnp.int32),
+        vmem((na, SIDES, nx, 2 * rows + FACTS, 128), BF16),
         vmem((2, 1, rows), jnp.int32),
         vmem((na, chunk, wide), F32),
         vmem((na, chunk, wide), F32),

time: 28.2 us -> 27.8 us (0.986)
  Pallas kernels: 27.4 us -> 27 us
    pallas_call x1, Pallas kernels: 26.7 us -> 26.2 us  [on_device(): pl.pallas_call(functools.partial(kernel, cfg), out_shape=tuple((pltpu.VME...]
where the time goes in v6:
time: 27.8 us; the launch traced here: 27.6 us
  Pallas kernels  27 us (97%)
  between operations  0.64 us (2%)
    pallas_call x1, Pallas kernels, on_device(): pl.pallas_call(functools.partial(kernel, cfg), out_shape=tuple((pltpu.VME...  26.2 us
    pallas_call x1, Pallas kernels, on_device(): pl.pallas_call(hand_over, out_shape=shapes, in_specs=[pl.BlockSpec(memory...  0.74 us

profile of v6, /device:TPU:0, one launch (start us, length us, event | category | flops | bytes accessed | tf_op | source)
XLA Modules:
  0.0 27.6 jit_solution(788584730379450889)
XLA Ops:
  0.6 26.2 %shard_map.85 = (f32[64,1024]{1,0:T(8,128)S(1)}, f32[64,128]{1,0:T(8,128)S(1)}, f32[64,128]{1,0:T(8,128)S(1)}) custom-call(bf16[64,1024]{1,0:T(8,128)(2,1)} %q_ref.1, bf16[64,128]{1,0:T(8,128)(2,1)} %k_ref.1, bf16[64,128]{1,0:T(8,128)(2,1)} %v_ref.1, bf16[64,1024]{1,0:T(8,128)(2,1)} %g_ref.1, s32[1,64]{1,0:T(1,128)} %bitcast.2, s32[1,64]{1,0:T(1,128)} %bitcast.3), custom_call_target="tpu_custom_call" | custom-call | flops 1342177280 | bytes 524288 | tf_op jit(solution)/shard_map/pallas_call | solution.py:361
  26.9 0.7 %shard_map.86 = (f32[64,1024]{1,0:T(8,128)}, f32[64,128]{1,0:T(8,128)}, f32[64,128]{1,0:T(8,128)}) custom-call(f32[64,1024]{1,0:T(8,128)S(1)} %get-tuple-element.6.refs_0_, f32[64,128]{1,0:T(8,128)S(1)} %get-tuple-element.7.refs_1_, f32[64,128]{1,0:T(8,128)S(1)} %get-tuple-element.8.refs_2_), custom_call_target="tpu_custom_call" | custom-call | tf_op jit(solution)/shard_map/pallas_call | solution.py:374

commit v7 on v6

--- a/solution.py
+++ b/solution.py
@@ -134,19 +134,26 @@
         a_copy(step).wait_recv()
         send_all(group_copies(step))
 
+    def lay_out(core):
+        base = core * lanes
+        for h in range(heads):
+            at = pl.ds(pl.multiple_of(base + h * rows, rows), rows)
+            qs[at, :] = raw[0, core, :, h * 128 : (h + 1) * 128]
+            gs[at, :] = raw[1, core, :, h * 128 : (h + 1) * 128]
+        span = pl.ds(pl.multiple_of(base, lanes), lanes)
+        qt[:, span] = jnp.transpose(qs[span, :])
+        gt[:, span] = jnp.transpose(gs[span, :])
+
     for one in own[4:]:
         one.wait()
+    lay_out(c)
+    if na > 1:
+        relay(1)
     for one in share + [id_share]:
         one.wait_recv()
-    for k in range(CORES):
-        for h in range(heads):
-            at = k * lanes + h * rows
-            qs[at : at + rows, :] = raw[0, k, :, h * 128 : (h + 1) * 128]
-            gs[at : at + rows, :] = raw[1, k, :, h * 128 : (h + 1) * 128]
-    for step in range(1, min(3, na)):
-        relay(step)
-    qt[...] = jnp.transpose(qs[...])
-    gt[...] = jnp.transpose(gs[...])
+    lay_out(1 - c)
+    if na > 2:
+        relay(2)
     both = [info_q[k] for k in range(CORES)]
     pos_q = jnp.concatenate([one[:, :rows] for one in both for _ in range(heads)], axis=1)
     doc_q = jnp.concatenate([one[:, rows : 2 * rows] for one in both for _ in range(heads)], axis=1)
@@ -231,7 +238,7 @@
             dscores = (probs * (dpbuf[step, :, cols] - row_dot[:, cols])).astype(BF16)
             sem["probs"][:, cols] = probs.astype(BF16)
             sem["dscores"][:, cols] = dscores
-        dk = dot(sem["dscores"][...], qs[...], 1, 0) * inv_root
+        dk = dot(sem["dscores"][...], qs[...], 1, 0)
         dv = dot(sem["probs"][...], gs[...], 1, 0)
         for which, one in enumerate((dk, dv)):
             one = one.reshape(SIDES, nx, rows, 128)
@@ -293,7 +300,7 @@
         return carry + a_in[step].astype(F32)
 
     done = lax.fori_loop(1, na, collect, a_own[0])
-    dk_ref[...] = done[0]
+    dk_ref[...] = done[0] * inv_root
     dv_ref[...] = done[1]
 
 

time: 27.8 us -> 28.4 us (1.022)
  Pallas kernels: 27 us -> 27.6 us
    pallas_call x1, Pallas kernels: 26.2 us -> 26.8 us  [on_device(): pl.pallas_call(functools.partial(kernel, cfg), out_shape=tuple((pltpu.VME...]
where the time goes in v7:
time: 28.4 us; the launch traced here: 28.2 us
  Pallas kernels  27.6 us (97%)
  between operations  0.64 us (2%)
    pallas_call x1, Pallas kernels, on_device(): pl.pallas_call(functools.partial(kernel, cfg), out_shape=tuple((pltpu.VME...  26.8 us
    pallas_call x1, Pallas kernels, on_device(): pl.pallas_call(hand_over, out_shape=shapes, in_specs=[pl.BlockSpec(memory...  0.74 us

profile of v7, /device:TPU:0, one launch (start us, length us, event | category | flops | bytes accessed | tf_op | source)
XLA Modules:
  0.0 28.2 jit_solution(12986449233218728774)
XLA Ops:
  0.6 26.8 %shard_map.85 = (f32[64,1024]{1,0:T(8,128)S(1)}, f32[64,128]{1,0:T(8,128)S(1)}, f32[64,128]{1,0:T(8,128)S(1)}) custom-call(bf16[64,1024]{1,0:T(8,128)(2,1)} %q_ref.1, bf16[64,128]{1,0:T(8,128)(2,1)} %k_ref.1, bf16[64,128]{1,0:T(8,128)(2,1)} %v_ref.1, bf16[64,1024]{1,0:T(8,128)(2,1)} %g_ref.1, s32[1,64]{1,0:T(1,128)} %bitcast.2, s32[1,64]{1,0:T(1,128)} %bitcast.3), custom_call_target="tpu_custom_call" | custom-call | flops 1342177280 | bytes 524288 | tf_op jit(solution)/shard_map/pallas_call | solution.py:368
  27.5 0.7 %shard_map.86 = (f32[64,1024]{1,0:T(8,128)}, f32[64,128]{1,0:T(8,128)}, f32[64,128]{1,0:T(8,128)}) custom-call(f32[64,1024]{1,0:T(8,128)S(1)} %get-tuple-element.6.refs_0_, f32[64,128]{1,0:T(8,128)S(1)} %get-tuple-element.7.refs_1_, f32[64,128]{1,0:T(8,128)S(1)} %get-tuple-element.8.refs_2_), custom_call_target="tpu_custom_call" | custom-call | tf_op jit(solution)/shard_map/pallas_call | solution.py:381

commit v8 on v7

--- a/solution.py
+++ b/solution.py
@@ -158,12 +158,18 @@
     pos_q = jnp.concatenate([one[:, :rows] for one in both for _ in range(heads)], axis=1)
     doc_q = jnp.concatenate([one[:, rows : 2 * rows] for one in both for _ in range(heads)], axis=1)
     wide = CORES * lanes
-    stats[0] = jnp.full((1, wide), NEG_BIG, F32)
-    stats[1] = jnp.zeros((1, wide), F32)
-    stats[2] = jnp.zeros((1, wide), F32)
+    for k in range(CORES):
+        stats[k, 0] = jnp.full((1, lanes), NEG_BIG, F32)
+        stats[k, 1] = jnp.zeros((1, lanes), F32)
+        stats[k, 2] = jnp.zeros((1, lanes), F32)
+    stats_in, finals = sem["stats_in"], sem["finals"]
+
+    def swap(k):
+        return copy(stats.at[k], stats_in.at[k], "stat", k, c_peer)
+
     dqt[...] = jnp.zeros(dqt.shape, F32)
 
-    tile = min(TILE, wide)
+    tile = min(TILE, lanes)
     tiles = [slice(t, t + tile) for t in range(0, wide, tile)]
     row_ids = lax.broadcasted_iota(jnp.int32, (rows, tile), 0).astype(F32)
 
@@ -187,7 +193,9 @@
         tables = [kv[at, b // nx, b % nx, 2 * rows :, :].astype(F32) for b in range(group)]
         for cols in tiles:
             scores = dot(keys, qt[:, cols], 1, 0)
-            old = stats[0, :, cols]
+            k = cols.start // lanes
+            local = slice(cols.start - k * lanes, cols.stop - k * lanes)
+            old = stats[k, 0, :, local]
             high = old
             for b in range(group):
                 row = lambda f: widen(tables[b][f : f + 1, :])
@@ -203,22 +211,27 @@
             dpbuf[step, :, cols] = dprobs
             fade = jnp.exp2(old - high)
             weights = jnp.exp2(sbuf[step, :, cols] - high)
-            stats[0, :, cols] = high
-            stats[1, :, cols] = stats[1, :, cols] * fade + jnp.sum(weights, axis=0, keepdims=True)
-            stats[2, :, cols] = stats[2, :, cols] * fade + jnp.sum(weights * dprobs, axis=0, keepdims=True)
+            stats[k, 0, :, local] = high
+            stats[k, 1, :, local] = stats[k, 1, :, local] * fade + jnp.sum(weights, axis=0, keepdims=True)
+            stats[k, 2, :, local] = stats[k, 2, :, local] * fade + jnp.sum(weights * dprobs, axis=0, keepdims=True)
+            if local.stop == lanes:
+
+                @pl.when(step == na - 1)
+                def _():
+                    swap(k).start()
+
         return carry
 
     lax.fori_loop(0, na, look, 0)
 
-    stats_in = sem["stats_in"]
-    swap = copy(stats, stats_in, "stat", 0, c_peer)
-    swap.start()
-    swap.wait_recv()
-    high = jnp.maximum(stats[0], stats_in[0])
-    here, there = jnp.exp2(stats[0] - high), jnp.exp2(stats_in[0] - high)
-    denom = stats[1] * here + stats_in[1] * there
-    log_total = high + jnp.log2(denom)
-    row_dot = (stats[2] * here + stats_in[2] * there) / denom
+    def finalize(k):
+        swap(k).wait_recv()
+        high = jnp.maximum(stats[k, 0], stats_in[k, 0])
+        here, there = jnp.exp2(stats[k, 0] - high), jnp.exp2(stats_in[k, 0] - high)
+        denom = stats[k, 1] * here + stats_in[k, 1] * there
+        span = slice(k * lanes, (k + 1) * lanes)
+        finals[0, :, span] = high + jnp.log2(denom)
+        finals[1, :, span] = (stats[k, 2] * here + stats_in[k, 2] * there) / denom
 
     def sum_copies(step):
         found = []
@@ -234,8 +247,14 @@
     def grads(step):
         keys_t = jnp.transpose(chunk_of(step, 0))
         for cols in tiles:
-            probs = jnp.exp2(sbuf[step, :, cols] - log_total[:, cols])
-            dscores = (probs * (dpbuf[step, :, cols] - row_dot[:, cols])).astype(BF16)
+            if cols.start % lanes == 0:
+
+                @pl.when(step == na - 1)
+                def _():
+                    finalize(cols.start // lanes)
+
+            probs = jnp.exp2(sbuf[step, :, cols] - finals[0, :, cols])
+            dscores = (probs * (dpbuf[step, :, cols] - finals[1, :, cols])).astype(BF16)
             sem["probs"][:, cols] = probs.astype(BF16)
             sem["dscores"][:, cols] = dscores
         dk = dot(sem["dscores"][...], qs[...], 1, 0)
@@ -281,7 +300,7 @@
         dq_ref[:, h * 128 : (h + 1) * 128] = dq[h * rows : (h + 1) * rows, :]
     second(0)
 
-    for one in first + share + [id_share] + [swap, swap_dq]:
+    for one in first + share + [id_share, swap(0), swap(1), swap_dq]:
         one.wait_send()
 
     def sent(step, carry):
@@ -326,15 +345,15 @@
     dma = pltpu.SemaphoreType.DMA
     vmem = pltpu.VMEM
     copies = {
-        "a": na, "g": na * group, "idq": 1, "qg": 2, "stat": 1,
+        "a": na, "g": na * group, "idq": 1, "qg": 2, "stat": CORES,
         "sum": na * group, "ra": na, "dq": 1,
     }
     names, tail = [], []
     for name, count in copies.items():
         names += ["s_" + name, "r_" + name]
         tail += [dma((count,)), dma((count,))]
-    names += ["own", "info_q", "stats_in", "probs", "dscores"]
-    tail += [dma((6,)), vmem((CORES, 1, 128), F32), vmem((3, 1, wide), F32)]
+    names += ["own", "info_q", "stats_in", "finals", "probs", "dscores"]
+    tail += [dma((6,)), vmem((CORES, 1, 128), F32), vmem((CORES, 3, 1, lanes), F32), vmem((2, 1, wide), F32)]
     tail += [vmem((chunk, wide), BF16), vmem((chunk, wide), BF16)]
     scratch = [
         vmem((2, CORES, rows, width), BF16),
@@ -346,7 +365,7 @@
         vmem((2, 1, rows), jnp.int32),
         vmem((na, chunk, wide), F32),
         vmem((na, chunk, wide), F32),
-        vmem((3, 1, wide), F32),
+        vmem((CORES, 3, 1, lanes), F32),
         vmem((CORES, 128, lanes), F32),
         vmem((128, lanes), F32),
         vmem((na, 2, SIDES, nx, rows, 128), F32),

time: 28.4 us -> 28.7 us (1.011)
  Pallas kernels: 27.6 us -> 27.9 us
    pallas_call x1, Pallas kernels: 26.8 us -> 27.2 us  [on_device(): pl.pallas_call(functools.partial(kernel, cfg), out_shape=tuple((pltpu.VME...]
where the time goes in v8:
time: 28.7 us; the launch traced here: 28.6 us
  Pallas kernels  27.9 us (97%)
  between operations  0.64 us (2%)
    pallas_call x1, Pallas kernels, on_device(): pl.pallas_call(functools.partial(kernel, cfg), out_shape=tuple((pltpu.VME...  27.2 us
    pallas_call x1, Pallas kernels, on_device(): pl.pallas_call(hand_over, out_shape=shapes, in_specs=[pl.BlockSpec(memory...  0.74 us

profile of v8, /device:TPU:0, one launch (start us, length us, event | category | flops | bytes accessed | tf_op | source)
XLA Modules:
  0.0 28.6 jit_solution(671186699816582491)
XLA Ops:
  0.6 27.2 %shard_map.85 = (f32[64,1024]{1,0:T(8,128)S(1)}, f32[64,128]{1,0:T(8,128)S(1)}, f32[64,128]{1,0:T(8,128)S(1)}) custom-call(bf16[64,1024]{1,0:T(8,128)(2,1)} %q_ref.1, bf16[64,128]{1,0:T(8,128)(2,1)} %k_ref.1, bf16[64,128]{1,0:T(8,128)(2,1)} %v_ref.1, bf16[64,1024]{1,0:T(8,128)(2,1)} %g_ref.1, s32[1,64]{1,0:T(1,128)} %bitcast.2, s32[1,64]{1,0:T(1,128)} %bitcast.3), custom_call_target="tpu_custom_call" | custom-call | flops 1342177280 | bytes 524288 | tf_op jit(solution)/shard_map/pallas_call | solution.py:387
  27.8 0.7 %shard_map.86 = (f32[64,1024]{1,0:T(8,128)}, f32[64,128]{1,0:T(8,128)}, f32[64,128]{1,0:T(8,128)}) custom-call(f32[64,1024]{1,0:T(8,128)S(1)} %get-tuple-element.6.refs_0_, f32[64,128]{1,0:T(8,128)S(1)} %get-tuple-element.7.refs_1_, f32[64,128]{1,0:T(8,128)S(1)} %get-tuple-element.8.refs_2_), custom_call_target="tpu_custom_call" | custom-call | tf_op jit(solution)/shard_map/pallas_call | solution.py:400
